TPU v7x, 512 devices: a whole 4x4x16 slice. The times are simulated.
512 devices in a mesh: lat: 64 (over z, y), lon: 8 (over x, core).
Axes of the slice: x: 4, y: 4, z: 16, core: 2. Of those that a mesh axis runs over, the one named last changes fastest.
Arguments:
- prior_sample_set: float32 [3, 80, 512, 1024], P(None, None, 'lat', 'lon'), may hold values from -6 to 6
- still_surface_thickness: float32 [512, 1024], P('lat', 'lon'), may hold values from 0.5 to 1.5
- lat_taper: float32 [32], replicated, may hold values from 0.1 to 1
- longitude_weight: float32 [256], replicated, may hold values from 0.1 to 1
- obs_cell: int32 [8192], P(('lat', 'lon')), may hold values from 0 to 524287, as said below
- obs_reach: int32 [8192], P(('lat', 'lon')), may hold values from 0 to 3
- obs_lon_reach: int32 [8192], P(('lat', 'lon')), may hold values from 0 to 1
- obs_batch: int32 [8192], P(('lat', 'lon')), may hold values from 0 to 1, as said below
- obs_value: float32 [8192], P(('lat', 'lon')), may hold values from -6 to 6
- obs_var: float32 [8192], P(('lat', 'lon')), may hold values from 0.2 to 2
Outputs:
- analysis: float32 [3, 80, 512, 1024], P(None, None, 'lat', 'lon')
Inputs may be any that keep to these rules, and one draw needn't show every extreme that they name: `obs_cell`: each observation lies in the cell block of the device that holds its slot (slots are laid out by device, latitude band slowest). `obs_batch`: in the slots of one device each batch holds at most 12 observations; in every draw some device holds exactly 12 of batch 0 and some device exactly 12 of batch 1.
All inputs are finite; a program needn't handle non-finite values.
Results may differ from a plain program's by a relative error of at most 0.0037.
Values may be sent and summed in bfloat16 or wider, within the bound.
A program may use at most 64 MiB of HBM per device.

v0:
```python
import jax
import jax.numpy as jnp
from jax import lax
from jax.sharding import PartitionSpec as P

REACH = 3
SUB = 4


TIMESTEP = 0.5
CORIOLIS_FACTOR = 0.3


def with_halo(block, sides, width, periodic):
    for axis, dim in sides:
        count = lax.axis_size(axis)
        forward = [(i, i + 1) for i in range(count - 1)]
        if periodic:
            forward.append((count - 1, 0))
        backward = [(target, source) for source, target in forward]
        low = lax.ppermute(
            lax.slice_in_dim(block, block.shape[dim] - width, None, axis=dim), axis, forward
        )
        high = lax.ppermute(lax.slice_in_dim(block, 0, width, axis=dim), axis, backward)
        block = jnp.concatenate([low, block, high], axis=dim)
    return block


def shifted(value, axis, steps):
    count = lax.axis_size(axis)
    pairs = [(source, (source + steps) % count) for source in range(count)]
    return lax.ppermute(value, axis, pairs)


def as_sent(value):
    return jax.tree.map(lambda a: a.astype(jnp.bfloat16) if a.dtype == jnp.float32 else a, value)


def shallow_step(physical_fields_vector, still_surface_thickness, rotation_frequency):
    height, eastward_speed, north_vel = (
        physical_fields_vector[0],
        physical_fields_vector[1],
        physical_fields_vector[2],
    )
    elevation_columns_count = with_halo(height, (("lon", 2),), 1, True)
    height_rows = with_halo(height, (("lat", 1),), 1, False)
    east_grad = 0.5 * (elevation_columns_count[:, :, 2:] - elevation_columns_count[:, :, :-2])
    north_grad = 0.5 * (height_rows[:, 2:, :] - height_rows[:, :-2, :])
    new_east = eastward_speed + TIMESTEP * (rotation_frequency * north_vel - east_grad)
    new_north = north_vel + TIMESTEP * (-rotation_frequency * eastward_speed - north_grad)
    east_ext = with_halo(new_east, (("lon", 2),), 1, True)
    north_ext = with_halo(new_north, (("lat", 1),), 1, False)
    diverge = 0.5 * (east_ext[:, :, 2:] - east_ext[:, :, :-2]) + 0.5 * (
        north_ext[:, 2:, :] - north_ext[:, :-2, :]
    )
    new_height = height - TIMESTEP * still_surface_thickness * diverge
    return jnp.stack([new_height, new_east, new_north])


def regress_window(
    state_dev,
    obs_piece,
    band_rows,
    sector_cols,
    own_band,
    own_sector,
    lon_count,
    lat_taper,
    longitude_weight,
    total_cols,
    rows_dev,
    cols_dev,
    members,
):
    obs_dev, coefs, labels = obs_piece
    obs_row = labels[0] // total_cols
    obs_col = labels[0] % total_cols
    lat_w = jnp.take(lat_taper, jnp.abs(band_rows[:, None] - obs_row[None, :]), mode="clip")
    col_dist = jnp.abs(sector_cols[:, None] - obs_col[None, :])
    col_dist = jnp.minimum(col_dist, total_cols - col_dist)
    lon_w = jnp.take(longitude_weight, col_dist, mode="clip")
    sector_dist = jnp.abs(own_sector - obs_col // cols_dev)
    sector_dist = jnp.minimum(sector_dist, lon_count - sector_dist)
    in_reach = (
        (jnp.abs(own_band - obs_row // rows_dev) <= labels[1]) & (sector_dist <= labels[2])
    ).astype(jnp.float32)
    locality = lat_w[:, None, :] * (lon_w * in_reach[None, :])[None, :, :]
    weights = (
        coefs[0][None, :].astype(jnp.float32)
        + coefs[1][None, :].astype(jnp.float32) * obs_dev.astype(jnp.float32)
    ).astype(jnp.bfloat16)
    results = []
    for field in range(3):
        covariance = jnp.einsum(
            "mij,mk->ijk", state_dev[field], obs_dev, preferred_element_type=jnp.float32
        )
        kalman_gain = (covariance * locality / (members - 1)).astype(jnp.bfloat16)
        results.append(
            jnp.einsum("ijk,mk->mij", kalman_gain, weights, preferred_element_type=jnp.float32)
        )
    return jnp.stack(results)


def per_device(
    prior_sample_set,
    still_surface_thickness,
    lat_taper,
    longitude_weight,
    obs_cell,
    obs_reach,
    obs_lon_reach,
    obs_batch,
    obs_value,
    obs_var,
):
    members = prior_sample_set.shape[1]
    rows_dev = prior_sample_set.shape[2]
    cols_dev = prior_sample_set.shape[3]
    lat_count = lax.axis_size("lat")
    lon_count = lax.axis_size("lon")
    lat_index = lax.axis_index("lat")
    lon_index = lax.axis_index("lon")
    total_rows = rows_dev * lat_count
    total_cols = cols_dev * lon_count
    band_rows = lat_index * rows_dev + jnp.arange(rows_dev)
    sector_cols = lon_index * cols_dev + jnp.arange(cols_dev)
    physical_fields_vector = prior_sample_set
    row_float = band_rows.astype(jnp.float32)
    rotation_frequency = (CORIOLIS_FACTOR * (2.0 * (row_float + 0.5) / total_rows - 1.0))[:, None]
    for substep in range(SUB):
        physical_fields_vector = shallow_step(
            physical_fields_vector, still_surface_thickness, rotation_frequency
        )
    local_index = (obs_cell // total_cols - lat_index * rows_dev) * cols_dev + (
        obs_cell % total_cols - lon_index * cols_dev
    )
    sector_offsets = [0]
    offset = 1
    for direction in (1, -1):
        sector_offsets.append(direction * offset)
    for batch_id in range(2):
        flat_height = physical_fields_vector[0].reshape(members, rows_dev * cols_dev)
        prior = jnp.take(flat_height, local_index, axis=1)
        live = (obs_batch == batch_id).astype(jnp.float32)
        ybar = jnp.mean(prior, axis=0)
        deviation = prior - ybar
        spread_sq = jnp.sum(deviation * deviation, axis=0) / (members - 1)
        total_var = spread_sq + obs_var
        obs_dev = (deviation * live).astype(jnp.bfloat16)
        shift_coef = live * (obs_value - ybar) / total_var
        spread_coef = -live / (jnp.sqrt(total_var) * (jnp.sqrt(obs_var) + jnp.sqrt(total_var)))
        coefs = jnp.stack([shift_coef, spread_coef]).astype(jnp.bfloat16)
        labels = jnp.stack([obs_cell, obs_reach, obs_lon_reach])
        sector_pieces = [(obs_dev, coefs, labels)]
        for offset in sector_offsets[1:]:
            sector_pieces.append(shifted((obs_dev, coefs, labels), "lon", offset))
        gathered = tuple(
            (
                jnp.concatenate([piece[member] for piece in sector_pieces], axis=1)
                for member in range(3)
            )
        )
        obs_pieces = [gathered]
        for offset in range(1, REACH + 1):
            for direction in (1, -1):
                obs_pieces.append(
                    shifted(
                        (gathered[0], gathered[1], as_sent(gathered[2])), "lat", direction * offset
                    )
                )
        joined = tuple(
            (
                jnp.concatenate([piece[member] for piece in obs_pieces], axis=1)
                for member in range(3)
            )
        )
        state_dev = (
            physical_fields_vector - jnp.mean(physical_fields_vector, axis=1, keepdims=True)
        ).astype(jnp.bfloat16)
        update = regress_window(
            state_dev,
            joined,
            band_rows,
            sector_cols,
            lat_index,
            lon_index,
            lon_count,
            lat_taper,
            longitude_weight,
            total_cols,
            rows_dev,
            cols_dev,
            members,
        )
        physical_fields_vector = physical_fields_vector + update
    return physical_fields_vector


def solution(mesh):
    return jax.shard_map(
        per_device,
        mesh=mesh,
        in_specs=(
            P(None, None, "lat", "lon"),
            P("lat", "lon"),
            P(),
            P(),
            P(("lat", "lon")),
            P(("lat", "lon")),
            P(("lat", "lon")),
            P(("lat", "lon")),
            P(("lat", "lon")),
            P(("lat", "lon")),
        ),
        out_specs=P(None, None, "lat", "lon"),
        check_vma=False,
    )
```

profile of v0, /device:TPU:384, one launch (start us, length us, event | category | flops | bytes accessed | tf_op | source)
XLA Modules:
  0.0 582.6 jit_solution(13448875394490671017)
XLA Ops:
  0.7 2.2 collective-permute-start.49
  4.9 2.2 collective-permute-done.48
  7.2 5.1 collective-permute-start.55
  12.4 1.9 collective-permute-start.54
  14.3 7.6 %collective-permute-start.53 = (s32[3,48]{1,0:T(4,128)S(1)}, s32[3,48]{1,0:T(4,128)S(1)}, u32[]{:S(2)}, u32[]{:S(2)}) collective-permute-start(s32[3,48]{1,0:T(4,128)S(1)} %pad_add_fusion.1), channel_id=1, source_target_pairs={{0,496},{8,504},{16,0},{24,8},{32,16},{40,24},{48,32},{56,40},{64,... | collective-permute-start | bytes 1736 | tf_op jit(solution)/shard_map/ppermute | solution.py:32
  21.9 1.9 collective-permute-start.52
  23.9 7.4 %collective-permute-start.51 = (s32[3,48]{1,0:T(4,128)S(1)}, s32[3,48]{1,0:T(4,128)S(1)}, u32[]{:S(2)}, u32[]{:S(2)}) collective-permute-start(s32[3,48]{1,0:T(4,128)S(1)} %pad_add_fusion.1), channel_id=1, source_target_pairs={{0,504},{8,0},{16,8},{24,16},{32,24},{40,32},{48,40},{56,48},{64,5... | collective-permute-start | bytes 1736 | tf_op jit(solution)/shard_map/ppermute | solution.py:32
  31.3 1.9 collective-permute-start.50
  33.2 7.2 %collective-permute-start.4 = (f32[80,1,128]{2,0,1:T(8,128)S(1)}, f32[80,1,128]{2,0,1:T(8,128)S(1)}, u32[]{:S(2)}, u32[]{:S(2)}) collective-permute-start(f32[80,1,128]{2,0,1:T(8,128)S(1)} %get-tuple-element.58), channel_id=1, source_target_pairs={{8,0},{16,8},{24,16},{32,24},{40,32},{48,40},{56,48},{64,56},{72,6... | collective-permute-start | bytes 122888 | tf_op jit(solution)/shard_map/ppermute | solution.py:24
  40.5 1.9 collective-permute-start.5
  43.0 4.0 collective-permute-done
  47.0 3.1 collective-permute-done.1
  50.6 7.2 %collective-permute-start.6 = (f32[80,1,128]{2,0,1:T(8,128)S(1)}, f32[80,1,128]{2,0,1:T(8,128)S(1)}, u32[]{:S(2)}, u32[]{:S(2)}) collective-permute-start(f32[80,1,128]{2,0,1:T(8,128)S(1)} %get-tuple-element.56), channel_id=1, source_target_pairs={{8,0},{16,8},{24,16},{32,24},{40,32},{48,40},{56,48},{64,56},{72,6... | collective-permute-start | bytes 122888 | tf_op jit(solution)/shard_map/ppermute | solution.py:24
  57.8 1.9 collective-permute-start.7
  60.5 4.1 collective-permute-done.2
  64.5 3.1 collective-permute-done.3
  68.2 7.2 %collective-permute-start.12 = (f32[80,1,128]{2,0,1:T(8,128)S(1)}, f32[80,1,128]{2,0,1:T(8,128)S(1)}, u32[]{:S(2)}, u32[]{:S(2)}) collective-permute-start(f32[80,1,128]{2,0,1:T(8,128)S(1)} %get-tuple-element.50), channel_id=1, source_target_pairs={{8,0},{16,8},{24,16},{32,24},{40,32},{48,40},{56,48},{64,56},{72,6... | collective-permute-start | bytes 122888 | tf_op jit(solution)/shard_map/ppermute | solution.py:24
  75.5 1.9 collective-permute-start.13
  78.2 3.8 collective-permute-done.8
  82.0 3.1 collective-permute-done.9
  85.5 7.2 %collective-permute-start.14 = (f32[80,1,128]{2,0,1:T(8,128)S(1)}, f32[80,1,128]{2,0,1:T(8,128)S(1)}, u32[]{:S(2)}, u32[]{:S(2)}) collective-permute-start(f32[80,1,128]{2,0,1:T(8,128)S(1)} %get-tuple-element.48), channel_id=1, source_target_pairs={{8,0},{16,8},{24,16},{32,24},{40,32},{48,40},{56,48},{64,56},{72,6... | collective-permute-start | bytes 122888 | tf_op jit(solution)/shard_map/ppermute | solution.py:24
  92.8 1.9 collective-permute-start.15
  95.4 4.1 collective-permute-done.10
  99.5 3.1 collective-permute-done.11
  103.1 7.2 %collective-permute-start.20 = (f32[80,1,128]{2,0,1:T(8,128)S(1)}, f32[80,1,128]{2,0,1:T(8,128)S(1)}, u32[]{:S(2)}, u32[]{:S(2)}) collective-permute-start(f32[80,1,128]{2,0,1:T(8,128)S(1)} %get-tuple-element.42), channel_id=1, source_target_pairs={{8,0},{16,8},{24,16},{32,24},{40,32},{48,40},{56,48},{64,56},{72,6... | collective-permute-start | bytes 122888 | tf_op jit(solution)/shard_map/ppermute | solution.py:24
  110.4 1.9 collective-permute-start.21
  112.9 265.3 %gather_fusion.1 = f32[43008]{0:T(1024)S(1)} fusion(f32[256]{0:T(256)S(1)} %copy-done, s32[43008]{0:T(1024)S(1)} %broadcast_clamp_fusion), kind=kCustom, calls=%fused_computation.3 | custom fusion | bytes 516096 | tf_op jit(solution)/shard_map/jit(_take)/gather | solution.py:81
  378.8 7.2 %collective-permute-start.22 = (f32[80,1,128]{2,0,1:T(8,128)S(1)}, f32[80,1,128]{2,0,1:T(8,128)S(1)}, u32[]{:S(2)}, u32[]{:S(2)}) collective-permute-start(f32[80,1,128]{2,0,1:T(8,128)S(1)} %get-tuple-element.40), channel_id=1, source_target_pairs={{8,0},{16,8},{24,16},{32,24},{40,32},{48,40},{56,48},{64,56},{72,6... | collective-permute-start | bytes 122888 | tf_op jit(solution)/shard_map/ppermute | solution.py:24
  386.0 1.9 collective-permute-start.23
  388.1 2.2 collective-permute-start.18
  390.3 4.6 collective-permute-done.18
  394.9 3.1 collective-permute-done.19
  398.5 7.0 %collective-permute-start.28 = (f32[80,1,128]{2,0,1:T(8,128)S(1)}, f32[80,1,128]{2,0,1:T(8,128)S(1)}, u32[]{:S(2)}, u32[]{:S(2)}) collective-permute-start(f32[80,1,128]{2,0,1:T(8,128)S(1)} %get-tuple-element.34), channel_id=1, source_target_pairs={{8,0},{16,8},{24,16},{32,24},{40,32},{48,40},{56,48},{64,56},{72,6... | collective-permute-start | bytes 122888 | tf_op jit(solution)/shard_map/ppermute | solution.py:24
  405.5 1.9 collective-permute-start.29
  408.1 3.9 collective-permute-done.24
  412.0 3.1 collective-permute-done.25
  415.6 7.2 %collective-permute-start.30 = (f32[80,1,128]{2,0,1:T(8,128)S(1)}, f32[80,1,128]{2,0,1:T(8,128)S(1)}, u32[]{:S(2)}, u32[]{:S(2)}) collective-permute-start(f32[80,1,128]{2,0,1:T(8,128)S(1)} %get-tuple-element.30), channel_id=1, source_target_pairs={{8,0},{16,8},{24,16},{32,24},{40,32},{48,40},{56,48},{64,56},{72,6... | collective-permute-start | bytes 122888 | tf_op jit(solution)/shard_map/ppermute | solution.py:24
  422.8 1.9 collective-permute-start.31
  425.5 15.5 %gather_fusion = f32[2688]{0:T(1024)S(1)} fusion(f32[32]{0:T(128)S(1)} %copy-done.1, s32[3072]{0:T(1024)S(1)} %pad_clamp_fusion), kind=kCustom, calls=%fused_computation.2 | custom fusion | bytes 32256 | tf_op jit(solution)/shard_map/jit(_take)/gather | solution.py:78
  442.5 2.5 collective-permute-start.33
  445.0 3.0 collective-permute-start.41
  449.4 2.9 collective-permute-done.40
  456.4 5.1 collective-permute-start.38
  461.5 4.3 collective-permute-start.37
  465.8 6.0 %collective-permute-start.36 = (bf16[2,48]{1,0:T(2,128)(2,1)S(1)}, bf16[2,48]{1,0:T(2,128)(2,1)S(1)}, u32[]{:S(2)}, u32[]{:S(2)}) collective-permute-start(bf16[2,48]{1,0:T(2,128)(2,1)S(1)} %pad_maximum_fusion.36), channel_id=1, source_target_pairs={{0,16},{8,24},{16,32},{24,40},{32,48},{40,56},{48,64},{56,72},{64,... | collective-permute-start | bytes 584 | tf_op jit(solution)/shard_map/ppermute | solution.py:32
  471.9 7.3 %collective-permute-start.35 = (bf16[2,48]{1,0:T(2,128)(2,1)S(1)}, bf16[2,48]{1,0:T(2,128)(2,1)S(1)}, u32[]{:S(2)}, u32[]{:S(2)}) collective-permute-start(bf16[2,48]{1,0:T(2,128)(2,1)S(1)} %pad_maximum_fusion.36), channel_id=1, source_target_pairs={{0,504},{8,0},{16,8},{24,16},{32,24},{40,32},{48,40},{56,48},{64,5... | collective-permute-start | bytes 584 | tf_op jit(solution)/shard_map/ppermute | solution.py:32
  481.2 6.8 %collective-permute-done.34 = bf16[2,48]{1,0:T(2,128)(2,1)S(1)} collective-permute-done((bf16[2,48]{1,0:T(2,128)(2,1)S(1)}, bf16[2,48]{1,0:T(2,128)(2,1)S(1)}, u32[]{:S(2)}, u32[]{:S(2)}) %collective-permute-start.34) | collective-permute-done | bytes 224 | tf_op jit(solution)/shard_map/ppermute | solution.py:32
  490.0 2.8 collective-permute-start.45
  492.7 4.6 collective-permute-start.44
  497.3 5.2 collective-permute-start.43
  504.5 7.0 %collective-permute-done.42 = bf16[80,48]{1,0:T(8,128)(2,1)S(1)} collective-permute-done((bf16[80,48]{1,0:T(8,128)(2,1)S(1)}, bf16[80,48]{1,0:T(8,128)(2,1)S(1)}, u32[]{:S(2)}, u32[]{:S(2)}) %collective-permute-start.42) | collective-permute-done | bytes 7712 | tf_op jit(solution)/shard_map/ppermute | solution.py:32
  515.4 2.5 collective-permute-start.65
  519.3 2.9 collective-permute-done.64
  522.4 1.9 collective-permute-start.71
  526.3 5.1 collective-permute-start.62
  531.4 3.7 collective-permute-start.61
  535.1 3.7 collective-permute-start.60
  538.8 7.8 %collective-permute-start.59 = (bf16[2,48]{1,0:T(2,128)(2,1)S(1)}, bf16[2,48]{1,0:T(2,128)(2,1)S(1)}, u32[]{:S(2)}, u32[]{:S(2)}) collective-permute-start(bf16[2,48]{1,0:T(2,128)(2,1)S(1)} %pad_maximum_fusion.38), channel_id=1, source_target_pairs={{0,504},{8,0},{16,8},{24,16},{32,24},{40,32},{48,40},{56,48},{64,5... | collective-permute-start | bytes 584 | tf_op jit(solution)/shard_map/ppermute | solution.py:32
  548.6 6.8 %collective-permute-done.58 = bf16[2,48]{1,0:T(2,128)(2,1)S(1)} collective-permute-done((bf16[2,48]{1,0:T(2,128)(2,1)S(1)}, bf16[2,48]{1,0:T(2,128)(2,1)S(1)}, u32[]{:S(2)}, u32[]{:S(2)}) %collective-permute-start.58) | collective-permute-done | bytes 224 | tf_op jit(solution)/shard_map/ppermute | solution.py:32
  557.4 2.8 collective-permute-start.69
  560.2 4.6 collective-permute-start.68
  564.8 5.2 collective-permute-start.67
  570.0 1.9 collective-permute-start.66
  572.0 7.0 %collective-permute-done.66 = bf16[80,48]{1,0:T(8,128)(2,1)S(1)} collective-permute-done((bf16[80,48]{1,0:T(8,128)(2,1)S(1)}, bf16[80,48]{1,0:T(8,128)(2,1)S(1)}, u32[]{:S(2)}, u32[]{:S(2)}) %collective-permute-start.66) | collective-permute-done | bytes 7712 | tf_op jit(solution)/shard_map/ppermute | solution.py:32
  (190 shorter events, 38.6 us)
Async XLA Ops:
  7.2 24.0 %collective-permute-start.55 = (s32[3,48]{1,0:T(4,128)S(1)}, s32[3,48]{1,0:T(4,128)S(1)}, u32[]{:S(2)}, u32[]{:S(2)}) collective-permute-start(s32[3,48]{1,0:T(4,128)S(1)} %pad_add_fusion.1), channel_id=1, source_target_pairs={{0,488},{8,496},{16,504},{24,0},{32,8},{40,16},{48,24},{56,32},{64... | collective-permute-start | bytes 1736 | tf_op jit(solution)/shard_map/ppermute | solution.py:32
  12.4 20.8 %collective-permute-start.54 = (s32[3,48]{1,0:T(4,128)S(1)}, s32[3,48]{1,0:T(4,128)S(1)}, u32[]{:S(2)}, u32[]{:S(2)}) collective-permute-start(s32[3,48]{1,0:T(4,128)S(1)} %pad_add_fusion.1), channel_id=1, source_target_pairs={{0,24},{8,32},{16,40},{24,48},{32,56},{40,64},{48,72},{56,80},{64,... | collective-permute-start | bytes 1736 | tf_op jit(solution)/shard_map/ppermute | solution.py:32
  14.3 26.2 %collective-permute-start.53 = (s32[3,48]{1,0:T(4,128)S(1)}, s32[3,48]{1,0:T(4,128)S(1)}, u32[]{:S(2)}, u32[]{:S(2)}) collective-permute-start(s32[3,48]{1,0:T(4,128)S(1)} %pad_add_fusion.1), channel_id=1, source_target_pairs={{0,496},{8,504},{16,0},{24,8},{32,16},{40,24},{48,32},{56,40},{64,... | collective-permute-start | bytes 1736 | tf_op jit(solution)/shard_map/ppermute | solution.py:32
  21.9 20.4 %collective-permute-start.52 = (s32[3,48]{1,0:T(4,128)S(1)}, s32[3,48]{1,0:T(4,128)S(1)}, u32[]{:S(2)}, u32[]{:S(2)}) collective-permute-start(s32[3,48]{1,0:T(4,128)S(1)} %pad_add_fusion.1), channel_id=1, source_target_pairs={{0,16},{8,24},{16,32},{24,40},{32,48},{40,56},{48,64},{56,72},{64,... | collective-permute-start | bytes 1736 | tf_op jit(solution)/shard_map/ppermute | solution.py:32
  23.9 18.5 %collective-permute-start.51 = (s32[3,48]{1,0:T(4,128)S(1)}, s32[3,48]{1,0:T(4,128)S(1)}, u32[]{:S(2)}, u32[]{:S(2)}) collective-permute-start(s32[3,48]{1,0:T(4,128)S(1)} %pad_add_fusion.1), channel_id=1, source_target_pairs={{0,504},{8,0},{16,8},{24,16},{32,24},{40,32},{48,40},{56,48},{64,5... | collective-permute-start | bytes 1736 | tf_op jit(solution)/shard_map/ppermute | solution.py:32
  31.3 11.7 %collective-permute-start.50 = (s32[3,48]{1,0:T(4,128)S(1)}, s32[3,48]{1,0:T(4,128)S(1)}, u32[]{:S(2)}, u32[]{:S(2)}) collective-permute-start(s32[3,48]{1,0:T(4,128)S(1)} %pad_add_fusion.1), channel_id=1, source_target_pairs={{0,8},{8,16},{16,24},{24,32},{32,40},{40,48},{48,56},{56,64},{64,7... | collective-permute-start | bytes 1736 | tf_op jit(solution)/shard_map/ppermute | solution.py:32
  33.2 17.0 %collective-permute-start.4 = (f32[80,1,128]{2,0,1:T(8,128)S(1)}, f32[80,1,128]{2,0,1:T(8,128)S(1)}, u32[]{:S(2)}, u32[]{:S(2)}) collective-permute-start(f32[80,1,128]{2,0,1:T(8,128)S(1)} %get-tuple-element.58), channel_id=1, source_target_pairs={{8,0},{16,8},{24,16},{32,24},{40,32},{48,40},{56,48},{64,56},{72,6... | collective-permute-start | bytes 122888 | tf_op jit(solution)/shard_map/ppermute | solution.py:24
  40.5 9.7 %collective-permute-start.5 = (f32[80,1,128]{2,0,1:T(8,128)S(1)}, f32[80,1,128]{2,0,1:T(8,128)S(1)}, u32[]{:S(2)}, u32[]{:S(2)}) collective-permute-start(f32[80,1,128]{2,0,1:T(8,128)S(1)} %get-tuple-element.59), channel_id=1, source_target_pairs={{0,8},{8,16},{16,24},{24,32},{32,40},{40,48},{48,56},{56,64},{64,7... | collective-permute-start | bytes 122888 | tf_op jit(solution)/shard_map/ppermute | solution.py:21
  42.4 4.6 collective-permute-start
  42.4 7.7 %collective-permute-start.1 = (f32[80,8,1]{2,0,1:T(8,128)S(1)}, f32[80,8,1]{2,0,1:T(8,128)S(1)}, u32[]{:S(2)}, u32[]{:S(2)}) collective-permute-start(f32[80,8,1]{2,0,1:T(8,128)S(1)} %get-tuple-element.55), channel_id=1, source_target_pairs={{0,1},{1,2},{2,3},{3,4},{4,5},{5,6},{6,7},{7,0},{8,9},{9,10},{10,1... | collective-permute-start | bytes 7688 | tf_op jit(solution)/shard_map/ppermute | solution.py:21
  50.6 17.1 %collective-permute-start.6 = (f32[80,1,128]{2,0,1:T(8,128)S(1)}, f32[80,1,128]{2,0,1:T(8,128)S(1)}, u32[]{:S(2)}, u32[]{:S(2)}) collective-permute-start(f32[80,1,128]{2,0,1:T(8,128)S(1)} %get-tuple-element.56), channel_id=1, source_target_pairs={{8,0},{16,8},{24,16},{32,24},{40,32},{48,40},{56,48},{64,56},{72,6... | collective-permute-start | bytes 122888 | tf_op jit(solution)/shard_map/ppermute | solution.py:24
  57.8 9.8 %collective-permute-start.7 = (f32[80,1,128]{2,0,1:T(8,128)S(1)}, f32[80,1,128]{2,0,1:T(8,128)S(1)}, u32[]{:S(2)}, u32[]{:S(2)}) collective-permute-start(f32[80,1,128]{2,0,1:T(8,128)S(1)} %get-tuple-element.57), channel_id=1, source_target_pairs={{0,8},{8,16},{16,24},{24,32},{32,40},{40,48},{48,56},{56,64},{64,7... | collective-permute-start | bytes 122888 | tf_op jit(solution)/shard_map/ppermute | solution.py:21
  60.0 7.7 %collective-permute-start.3 = (f32[80,8,1]{2,0,1:T(8,128)S(1)}, f32[80,8,1]{2,0,1:T(8,128)S(1)}, u32[]{:S(2)}, u32[]{:S(2)}) collective-permute-start(f32[80,8,1]{2,0,1:T(8,128)S(1)} %get-tuple-element.53), channel_id=1, source_target_pairs={{0,1},{1,2},{2,3},{3,4},{4,5},{5,6},{6,7},{7,0},{8,9},{9,10},{10,1... | collective-permute-start | bytes 7688 | tf_op jit(solution)/shard_map/ppermute | solution.py:21
  68.2 16.9 %collective-permute-start.12 = (f32[80,1,128]{2,0,1:T(8,128)S(1)}, f32[80,1,128]{2,0,1:T(8,128)S(1)}, u32[]{:S(2)}, u32[]{:S(2)}) collective-permute-start(f32[80,1,128]{2,0,1:T(8,128)S(1)} %get-tuple-element.50), channel_id=1, source_target_pairs={{8,0},{16,8},{24,16},{32,24},{40,32},{48,40},{56,48},{64,56},{72,6... | collective-permute-start | bytes 122888 | tf_op jit(solution)/shard_map/ppermute | solution.py:24
  75.5 9.7 %collective-permute-start.13 = (f32[80,1,128]{2,0,1:T(8,128)S(1)}, f32[80,1,128]{2,0,1:T(8,128)S(1)}, u32[]{:S(2)}, u32[]{:S(2)}) collective-permute-start(f32[80,1,128]{2,0,1:T(8,128)S(1)} %get-tuple-element.51), channel_id=1, source_target_pairs={{0,8},{8,16},{16,24},{24,32},{32,40},{40,48},{48,56},{56,64},{64,7... | collective-permute-start | bytes 122888 | tf_op jit(solution)/shard_map/ppermute | solution.py:21
  77.4 4.6 collective-permute-start.8
  77.4 7.7 %collective-permute-start.9 = (f32[80,8,1]{2,0,1:T(8,128)S(1)}, f32[80,8,1]{2,0,1:T(8,128)S(1)}, u32[]{:S(2)}, u32[]{:S(2)}) collective-permute-start(f32[80,8,1]{2,0,1:T(8,128)S(1)} %get-tuple-element.47), channel_id=1, source_target_pairs={{0,1},{1,2},{2,3},{3,4},{4,5},{5,6},{6,7},{7,0},{8,9},{9,10},{10,1... | collective-permute-start | bytes 7688 | tf_op jit(solution)/shard_map/ppermute | solution.py:21
  85.5 17.1 %collective-permute-start.14 = (f32[80,1,128]{2,0,1:T(8,128)S(1)}, f32[80,1,128]{2,0,1:T(8,128)S(1)}, u32[]{:S(2)}, u32[]{:S(2)}) collective-permute-start(f32[80,1,128]{2,0,1:T(8,128)S(1)} %get-tuple-element.48), channel_id=1, source_target_pairs={{8,0},{16,8},{24,16},{32,24},{40,32},{48,40},{56,48},{64,56},{72,6... | collective-permute-start | bytes 122888 | tf_op jit(solution)/shard_map/ppermute | solution.py:24
  92.8 9.8 %collective-permute-start.15 = (f32[80,1,128]{2,0,1:T(8,128)S(1)}, f32[80,1,128]{2,0,1:T(8,128)S(1)}, u32[]{:S(2)}, u32[]{:S(2)}) collective-permute-start(f32[80,1,128]{2,0,1:T(8,128)S(1)} %get-tuple-element.49), channel_id=1, source_target_pairs={{0,8},{8,16},{16,24},{24,32},{32,40},{40,48},{48,56},{56,64},{64,7... | collective-permute-start | bytes 122888 | tf_op jit(solution)/shard_map/ppermute | solution.py:21
  94.9 7.7 %collective-permute-start.11 = (f32[80,8,1]{2,0,1:T(8,128)S(1)}, f32[80,8,1]{2,0,1:T(8,128)S(1)}, u32[]{:S(2)}, u32[]{:S(2)}) collective-permute-start(f32[80,8,1]{2,0,1:T(8,128)S(1)} %get-tuple-element.45), channel_id=1, source_target_pairs={{0,1},{1,2},{2,3},{3,4},{4,5},{5,6},{6,7},{7,0},{8,9},{9,10},{10,1... | collective-permute-start | bytes 7688 | tf_op jit(solution)/shard_map/ppermute | solution.py:21
  103.1 275.2 %collective-permute-start.20 = (f32[80,1,128]{2,0,1:T(8,128)S(1)}, f32[80,1,128]{2,0,1:T(8,128)S(1)}, u32[]{:S(2)}, u32[]{:S(2)}) collective-permute-start(f32[80,1,128]{2,0,1:T(8,128)S(1)} %get-tuple-element.42), channel_id=1, source_target_pairs={{8,0},{16,8},{24,16},{32,24},{40,32},{48,40},{56,48},{64,56},{72,6... | collective-permute-start | bytes 122888 | tf_op jit(solution)/shard_map/ppermute | solution.py:24
  110.4 268.0 %collective-permute-start.21 = (f32[80,1,128]{2,0,1:T(8,128)S(1)}, f32[80,1,128]{2,0,1:T(8,128)S(1)}, u32[]{:S(2)}, u32[]{:S(2)}) collective-permute-start(f32[80,1,128]{2,0,1:T(8,128)S(1)} %get-tuple-element.43), channel_id=1, source_target_pairs={{0,8},{8,16},{16,24},{24,32},{32,40},{40,48},{48,56},{56,64},{64,7... | collective-permute-start | bytes 122888 | tf_op jit(solution)/shard_map/ppermute | solution.py:21
  112.3 266.0 %collective-permute-start.16 = (f32[80,8,1]{2,0,1:T(8,128)S(1)}, f32[80,8,1]{2,0,1:T(8,128)S(1)}, u32[]{:S(2)}, u32[]{:S(2)}) collective-permute-start(f32[80,8,1]{2,0,1:T(8,128)S(1)} %get-tuple-element.38), channel_id=1, source_target_pairs={{1,0},{2,1},{3,2},{4,3},{5,4},{6,5},{7,6},{0,7},{9,8},{10,9},{11,1... | collective-permute-start | bytes 7688 | tf_op jit(solution)/shard_map/ppermute | solution.py:24
  112.3 266.0 %collective-permute-start.17 = (f32[80,8,1]{2,0,1:T(8,128)S(1)}, f32[80,8,1]{2,0,1:T(8,128)S(1)}, u32[]{:S(2)}, u32[]{:S(2)}) collective-permute-start(f32[80,8,1]{2,0,1:T(8,128)S(1)} %get-tuple-element.39), channel_id=1, source_target_pairs={{0,1},{1,2},{2,3},{3,4},{4,5},{5,6},{6,7},{7,0},{8,9},{9,10},{10,1... | collective-permute-start | bytes 7688 | tf_op jit(solution)/shard_map/ppermute | solution.py:21
  378.8 19.3 %collective-permute-start.22 = (f32[80,1,128]{2,0,1:T(8,128)S(1)}, f32[80,1,128]{2,0,1:T(8,128)S(1)}, u32[]{:S(2)}, u32[]{:S(2)}) collective-permute-start(f32[80,1,128]{2,0,1:T(8,128)S(1)} %get-tuple-element.40), channel_id=1, source_target_pairs={{8,0},{16,8},{24,16},{32,24},{40,32},{48,40},{56,48},{64,56},{72,6... | collective-permute-start | bytes 122888 | tf_op jit(solution)/shard_map/ppermute | solution.py:24
  386.0 12.0 %collective-permute-start.23 = (f32[80,1,128]{2,0,1:T(8,128)S(1)}, f32[80,1,128]{2,0,1:T(8,128)S(1)}, u32[]{:S(2)}, u32[]{:S(2)}) collective-permute-start(f32[80,1,128]{2,0,1:T(8,128)S(1)} %get-tuple-element.41), channel_id=1, source_target_pairs={{0,8},{8,16},{16,24},{24,32},{32,40},{40,48},{48,56},{56,64},{64,7... | collective-permute-start | bytes 122888 | tf_op jit(solution)/shard_map/ppermute | solution.py:21
  388.1 6.8 %collective-permute-start.18 = (f32[80,8,1]{2,0,1:T(8,128)S(1)}, f32[80,8,1]{2,0,1:T(8,128)S(1)}, u32[]{:S(2)}, u32[]{:S(2)}) collective-permute-start(f32[80,8,1]{2,0,1:T(8,128)S(1)} %get-tuple-element.36), channel_id=1, source_target_pairs={{1,0},{2,1},{3,2},{4,3},{5,4},{6,5},{7,6},{0,7},{9,8},{10,9},{11,1... | collective-permute-start | bytes 7688 | tf_op jit(solution)/shard_map/ppermute | solution.py:24
  390.3 7.7 %collective-permute-start.19 = (f32[80,8,1]{2,0,1:T(8,128)S(1)}, f32[80,8,1]{2,0,1:T(8,128)S(1)}, u32[]{:S(2)}, u32[]{:S(2)}) collective-permute-start(f32[80,8,1]{2,0,1:T(8,128)S(1)} %get-tuple-element.37), channel_id=1, source_target_pairs={{0,1},{1,2},{2,3},{3,4},{4,5},{5,6},{6,7},{7,0},{8,9},{9,10},{10,1... | collective-permute-start | bytes 7688 | tf_op jit(solution)/shard_map/ppermute | solution.py:21
  398.5 16.6 %collective-permute-start.28 = (f32[80,1,128]{2,0,1:T(8,128)S(1)}, f32[80,1,128]{2,0,1:T(8,128)S(1)}, u32[]{:S(2)}, u32[]{:S(2)}) collective-permute-start(f32[80,1,128]{2,0,1:T(8,128)S(1)} %get-tuple-element.34), channel_id=1, source_target_pairs={{8,0},{16,8},{24,16},{32,24},{40,32},{48,40},{56,48},{64,56},{72,6... | collective-permute-start | bytes 122888 | tf_op jit(solution)/shard_map/ppermute | solution.py:24
  405.5 9.7 %collective-permute-start.29 = (f32[80,1,128]{2,0,1:T(8,128)S(1)}, f32[80,1,128]{2,0,1:T(8,128)S(1)}, u32[]{:S(2)}, u32[]{:S(2)}) collective-permute-start(f32[80,1,128]{2,0,1:T(8,128)S(1)} %get-tuple-element.35), channel_id=1, source_target_pairs={{0,8},{8,16},{16,24},{24,32},{32,40},{40,48},{48,56},{56,64},{64,7... | collective-permute-start | bytes 122888 | tf_op jit(solution)/shard_map/ppermute | solution.py:21
  407.4 4.6 collective-permute-start.24
  407.5 7.7 %collective-permute-start.25 = (f32[80,8,1]{2,0,1:T(8,128)S(1)}, f32[80,8,1]{2,0,1:T(8,128)S(1)}, u32[]{:S(2)}, u32[]{:S(2)}) collective-permute-start(f32[80,8,1]{2,0,1:T(8,128)S(1)} %get-tuple-element.33), channel_id=1, source_target_pairs={{0,1},{1,2},{2,3},{3,4},{4,5},{5,6},{6,7},{7,0},{8,9},{9,10},{10,1... | collective-permute-start | bytes 7688 | tf_op jit(solution)/shard_map/ppermute | solution.py:21
  415.6 25.6 %collective-permute-start.30 = (f32[80,1,128]{2,0,1:T(8,128)S(1)}, f32[80,1,128]{2,0,1:T(8,128)S(1)}, u32[]{:S(2)}, u32[]{:S(2)}) collective-permute-start(f32[80,1,128]{2,0,1:T(8,128)S(1)} %get-tuple-element.30), channel_id=1, source_target_pairs={{8,0},{16,8},{24,16},{32,24},{40,32},{48,40},{56,48},{64,56},{72,6... | collective-permute-start | bytes 122888 | tf_op jit(solution)/shard_map/ppermute | solution.py:24
  422.8 18.3 %collective-permute-start.31 = (f32[80,1,128]{2,0,1:T(8,128)S(1)}, f32[80,1,128]{2,0,1:T(8,128)S(1)}, u32[]{:S(2)}, u32[]{:S(2)}) collective-permute-start(f32[80,1,128]{2,0,1:T(8,128)S(1)} %get-tuple-element.31), channel_id=1, source_target_pairs={{0,8},{8,16},{16,24},{24,32},{32,40},{40,48},{48,56},{56,64},{64,7... | collective-permute-start | bytes 122888 | tf_op jit(solution)/shard_map/ppermute | solution.py:21
  424.9 16.2 %collective-permute-start.26 = (f32[80,8,1]{2,0,1:T(8,128)S(1)}, f32[80,8,1]{2,0,1:T(8,128)S(1)}, u32[]{:S(2)}, u32[]{:S(2)}) collective-permute-start(f32[80,8,1]{2,0,1:T(8,128)S(1)} %get-tuple-element.28), channel_id=1, source_target_pairs={{1,0},{2,1},{3,2},{4,3},{5,4},{6,5},{7,6},{0,7},{9,8},{10,9},{11,1... | collective-permute-start | bytes 7688 | tf_op jit(solution)/shard_map/ppermute | solution.py:24
  425.0 16.2 %collective-permute-start.27 = (f32[80,8,1]{2,0,1:T(8,128)S(1)}, f32[80,8,1]{2,0,1:T(8,128)S(1)}, u32[]{:S(2)}, u32[]{:S(2)}) collective-permute-start(f32[80,8,1]{2,0,1:T(8,128)S(1)} %get-tuple-element.29), channel_id=1, source_target_pairs={{0,1},{1,2},{2,3},{3,4},{4,5},{5,6},{6,7},{7,0},{8,9},{9,10},{10,1... | collective-permute-start | bytes 7688 | tf_op jit(solution)/shard_map/ppermute | solution.py:21
  442.5 11.9 %collective-permute-start.33 = (bf16[2,16]{1,0:T(2,128)(2,1)S(1)}, bf16[2,16]{1,0:T(2,128)(2,1)S(1)}, u32[]{:S(2)}, u32[]{:S(2)}) collective-permute-start(bf16[2,16]{1,0:T(2,128)(2,1)S(1)} %pad_maximum_fusion.35), channel_id=1, source_target_pairs={{0,7},{1,0},{2,1},{3,2},{4,3},{5,4},{6,5},{7,6},{8,15},{9,8},{10,9... | collective-permute-start | bytes 200 | tf_op jit(solution)/shard_map/ppermute | solution.py:32
  445.0 9.4 %collective-permute-start.32 = (bf16[2,16]{1,0:T(2,128)(2,1)S(1)}, bf16[2,16]{1,0:T(2,128)(2,1)S(1)}, u32[]{:S(2)}, u32[]{:S(2)}) collective-permute-start(bf16[2,16]{1,0:T(2,128)(2,1)S(1)} %pad_maximum_fusion.35), channel_id=1, source_target_pairs={{0,1},{1,2},{2,3},{3,4},{4,5},{5,6},{6,7},{7,0},{8,9},{9,10},{10,1... | collective-permute-start | bytes 200 | tf_op jit(solution)/shard_map/ppermute | solution.py:32
  452.5 50.1 %collective-permute-start.47 = (bf16[80,48]{1,0:T(8,128)(2,1)S(1)}, bf16[80,48]{1,0:T(8,128)(2,1)S(1)}, u32[]{:S(2)}, u32[]{:S(2)}) collective-permute-start(bf16[80,48]{1,0:T(8,128)(2,1)S(1)} %pad_maximum_fusion.33), channel_id=1, source_target_pairs={{0,488},{8,496},{16,504},{24,0},{32,8},{40,16},{48,24},{56,32},{64... | collective-permute-start | bytes 23048 | tf_op jit(solution)/shard_map/ppermute | solution.py:32
  454.5 17.4 %collective-permute-start.39 = (bf16[2,48]{1,0:T(2,128)(2,1)S(1)}, bf16[2,48]{1,0:T(2,128)(2,1)S(1)}, u32[]{:S(2)}, u32[]{:S(2)}) collective-permute-start(bf16[2,48]{1,0:T(2,128)(2,1)S(1)} %pad_maximum_fusion.36), channel_id=1, source_target_pairs={{0,488},{8,496},{16,504},{24,0},{32,8},{40,16},{48,24},{56,32},{64... | collective-permute-start | bytes 584 | tf_op jit(solution)/shard_map/ppermute | solution.py:32
  456.4 22.8 %collective-permute-start.38 = (bf16[2,48]{1,0:T(2,128)(2,1)S(1)}, bf16[2,48]{1,0:T(2,128)(2,1)S(1)}, u32[]{:S(2)}, u32[]{:S(2)}) collective-permute-start(bf16[2,48]{1,0:T(2,128)(2,1)S(1)} %pad_maximum_fusion.36), channel_id=1, source_target_pairs={{0,24},{8,32},{16,40},{24,48},{32,56},{40,64},{48,72},{56,80},{64,... | collective-permute-start | bytes 584 | tf_op jit(solution)/shard_map/ppermute | solution.py:32
  461.5 19.6 %collective-permute-start.37 = (bf16[2,48]{1,0:T(2,128)(2,1)S(1)}, bf16[2,48]{1,0:T(2,128)(2,1)S(1)}, u32[]{:S(2)}, u32[]{:S(2)}) collective-permute-start(bf16[2,48]{1,0:T(2,128)(2,1)S(1)} %pad_maximum_fusion.36), channel_id=1, source_target_pairs={{0,496},{8,504},{16,0},{24,8},{32,16},{40,24},{48,32},{56,40},{64,... | collective-permute-start | bytes 584 | tf_op jit(solution)/shard_map/ppermute | solution.py:32
  465.8 15.3 %collective-permute-start.36 = (bf16[2,48]{1,0:T(2,128)(2,1)S(1)}, bf16[2,48]{1,0:T(2,128)(2,1)S(1)}, u32[]{:S(2)}, u32[]{:S(2)}) collective-permute-start(bf16[2,48]{1,0:T(2,128)(2,1)S(1)} %pad_maximum_fusion.36), channel_id=1, source_target_pairs={{0,16},{8,24},{16,32},{24,40},{32,48},{40,56},{48,64},{56,72},{64,... | collective-permute-start | bytes 584 | tf_op jit(solution)/shard_map/ppermute | solution.py:32
  471.9 9.3 %collective-permute-start.35 = (bf16[2,48]{1,0:T(2,128)(2,1)S(1)}, bf16[2,48]{1,0:T(2,128)(2,1)S(1)}, u32[]{:S(2)}, u32[]{:S(2)}) collective-permute-start(bf16[2,48]{1,0:T(2,128)(2,1)S(1)} %pad_maximum_fusion.36), channel_id=1, source_target_pairs={{0,504},{8,0},{16,8},{24,16},{32,24},{40,32},{48,40},{56,48},{64,5... | collective-permute-start | bytes 584 | tf_op jit(solution)/shard_map/ppermute | solution.py:32
  479.2 8.8 %collective-permute-start.34 = (bf16[2,48]{1,0:T(2,128)(2,1)S(1)}, bf16[2,48]{1,0:T(2,128)(2,1)S(1)}, u32[]{:S(2)}, u32[]{:S(2)}) collective-permute-start(bf16[2,48]{1,0:T(2,128)(2,1)S(1)} %pad_maximum_fusion.36), channel_id=1, source_target_pairs={{0,8},{8,16},{16,24},{24,32},{32,40},{40,48},{48,56},{56,64},{64,7... | collective-permute-start | bytes 584 | tf_op jit(solution)/shard_map/ppermute | solution.py:32
  488.0 16.4 %collective-permute-start.46 = (bf16[80,48]{1,0:T(8,128)(2,1)S(1)}, bf16[80,48]{1,0:T(8,128)(2,1)S(1)}, u32[]{:S(2)}, u32[]{:S(2)}) collective-permute-start(bf16[80,48]{1,0:T(8,128)(2,1)S(1)} %pad_maximum_fusion.33), channel_id=1, source_target_pairs={{0,24},{8,32},{16,40},{24,48},{32,56},{40,64},{48,72},{56,80},{64,... | collective-permute-start | bytes 23048 | tf_op jit(solution)/shard_map/ppermute | solution.py:32
  490.0 14.5 %collective-permute-start.45 = (bf16[80,48]{1,0:T(8,128)(2,1)S(1)}, bf16[80,48]{1,0:T(8,128)(2,1)S(1)}, u32[]{:S(2)}, u32[]{:S(2)}) collective-permute-start(bf16[80,48]{1,0:T(8,128)(2,1)S(1)} %pad_maximum_fusion.33), channel_id=1, source_target_pairs={{0,496},{8,504},{16,0},{24,8},{32,16},{40,24},{48,32},{56,40},{64,... | collective-permute-start | bytes 23048 | tf_op jit(solution)/shard_map/ppermute | solution.py:32
  492.7 11.8 %collective-permute-start.44 = (bf16[80,48]{1,0:T(8,128)(2,1)S(1)}, bf16[80,48]{1,0:T(8,128)(2,1)S(1)}, u32[]{:S(2)}, u32[]{:S(2)}) collective-permute-start(bf16[80,48]{1,0:T(8,128)(2,1)S(1)} %pad_maximum_fusion.33), channel_id=1, source_target_pairs={{0,16},{8,24},{16,32},{24,40},{32,48},{40,56},{48,64},{56,72},{64,... | collective-permute-start | bytes 23048 | tf_op jit(solution)/shard_map/ppermute | solution.py:32
  497.3 7.2 %collective-permute-start.43 = (bf16[80,48]{1,0:T(8,128)(2,1)S(1)}, bf16[80,48]{1,0:T(8,128)(2,1)S(1)}, u32[]{:S(2)}, u32[]{:S(2)}) collective-permute-start(bf16[80,48]{1,0:T(8,128)(2,1)S(1)} %pad_maximum_fusion.33), channel_id=1, source_target_pairs={{0,504},{8,0},{16,8},{24,16},{32,24},{40,32},{48,40},{56,48},{64,5... | collective-permute-start | bytes 23048 | tf_op jit(solution)/shard_map/ppermute | solution.py:32
  502.5 9.0 %collective-permute-start.42 = (bf16[80,48]{1,0:T(8,128)(2,1)S(1)}, bf16[80,48]{1,0:T(8,128)(2,1)S(1)}, u32[]{:S(2)}, u32[]{:S(2)}) collective-permute-start(bf16[80,48]{1,0:T(8,128)(2,1)S(1)} %pad_maximum_fusion.33), channel_id=1, source_target_pairs={{0,8},{8,16},{16,24},{24,32},{32,40},{40,48},{48,56},{56,64},{64,7... | collective-permute-start | bytes 23048 | tf_op jit(solution)/shard_map/ppermute | solution.py:32
  514.9 9.4 %collective-permute-start.57 = (bf16[2,16]{1,0:T(2,128)(2,1)S(1)}, bf16[2,16]{1,0:T(2,128)(2,1)S(1)}, u32[]{:S(2)}, u32[]{:S(2)}) collective-permute-start(bf16[2,16]{1,0:T(2,128)(2,1)S(1)} %pad_maximum_fusion.37), channel_id=1, source_target_pairs={{0,7},{1,0},{2,1},{3,2},{4,3},{5,4},{6,5},{7,6},{8,15},{9,8},{10,9... | collective-permute-start | bytes 200 | tf_op jit(solution)/shard_map/ppermute | solution.py:32
  514.9 9.4 %collective-permute-start.56 = (bf16[2,16]{1,0:T(2,128)(2,1)S(1)}, bf16[2,16]{1,0:T(2,128)(2,1)S(1)}, u32[]{:S(2)}, u32[]{:S(2)}) collective-permute-start(bf16[2,16]{1,0:T(2,128)(2,1)S(1)} %pad_maximum_fusion.37), channel_id=1, source_target_pairs={{0,1},{1,2},{2,3},{3,4},{4,5},{5,6},{6,7},{7,0},{8,9},{9,10},{10,1... | collective-permute-start | bytes 200 | tf_op jit(solution)/shard_map/ppermute | solution.py:32
  522.4 47.6 %collective-permute-start.71 = (bf16[80,48]{1,0:T(8,128)(2,1)S(1)}, bf16[80,48]{1,0:T(8,128)(2,1)S(1)}, u32[]{:S(2)}, u32[]{:S(2)}) collective-permute-start(bf16[80,48]{1,0:T(8,128)(2,1)S(1)} %pad_maximum_fusion.34), channel_id=1, source_target_pairs={{0,488},{8,496},{16,504},{24,0},{32,8},{40,16},{48,24},{56,32},{64... | collective-permute-start | bytes 23048 | tf_op jit(solution)/shard_map/ppermute | solution.py:32
  524.4 14.4 %collective-permute-start.63 = (bf16[2,48]{1,0:T(2,128)(2,1)S(1)}, bf16[2,48]{1,0:T(2,128)(2,1)S(1)}, u32[]{:S(2)}, u32[]{:S(2)}) collective-permute-start(bf16[2,48]{1,0:T(2,128)(2,1)S(1)} %pad_maximum_fusion.38), channel_id=1, source_target_pairs={{0,488},{8,496},{16,504},{24,0},{32,8},{40,16},{48,24},{56,32},{64... | collective-permute-start | bytes 584 | tf_op jit(solution)/shard_map/ppermute | solution.py:32
  526.3 20.4 %collective-permute-start.62 = (bf16[2,48]{1,0:T(2,128)(2,1)S(1)}, bf16[2,48]{1,0:T(2,128)(2,1)S(1)}, u32[]{:S(2)}, u32[]{:S(2)}) collective-permute-start(bf16[2,48]{1,0:T(2,128)(2,1)S(1)} %pad_maximum_fusion.38), channel_id=1, source_target_pairs={{0,24},{8,32},{16,40},{24,48},{32,56},{40,64},{48,72},{56,80},{64,... | collective-permute-start | bytes 584 | tf_op jit(solution)/shard_map/ppermute | solution.py:32
  531.4 17.1 %collective-permute-start.61 = (bf16[2,48]{1,0:T(2,128)(2,1)S(1)}, bf16[2,48]{1,0:T(2,128)(2,1)S(1)}, u32[]{:S(2)}, u32[]{:S(2)}) collective-permute-start(bf16[2,48]{1,0:T(2,128)(2,1)S(1)} %pad_maximum_fusion.38), channel_id=1, source_target_pairs={{0,496},{8,504},{16,0},{24,8},{32,16},{40,24},{48,32},{56,40},{64,... | collective-permute-start | bytes 584 | tf_op jit(solution)/shard_map/ppermute | solution.py:32
  535.1 13.5 %collective-permute-start.60 = (bf16[2,48]{1,0:T(2,128)(2,1)S(1)}, bf16[2,48]{1,0:T(2,128)(2,1)S(1)}, u32[]{:S(2)}, u32[]{:S(2)}) collective-permute-start(bf16[2,48]{1,0:T(2,128)(2,1)S(1)} %pad_maximum_fusion.38), channel_id=1, source_target_pairs={{0,16},{8,24},{16,32},{24,40},{32,48},{40,56},{48,64},{56,72},{64,... | collective-permute-start | bytes 584 | tf_op jit(solution)/shard_map/ppermute | solution.py:32
  538.8 9.8 %collective-permute-start.59 = (bf16[2,48]{1,0:T(2,128)(2,1)S(1)}, bf16[2,48]{1,0:T(2,128)(2,1)S(1)}, u32[]{:S(2)}, u32[]{:S(2)}) collective-permute-start(bf16[2,48]{1,0:T(2,128)(2,1)S(1)} %pad_maximum_fusion.38), channel_id=1, source_target_pairs={{0,504},{8,0},{16,8},{24,16},{32,24},{40,32},{48,40},{56,48},{64,5... | collective-permute-start | bytes 584 | tf_op jit(solution)/shard_map/ppermute | solution.py:32
  546.7 8.8 %collective-permute-start.58 = (bf16[2,48]{1,0:T(2,128)(2,1)S(1)}, bf16[2,48]{1,0:T(2,128)(2,1)S(1)}, u32[]{:S(2)}, u32[]{:S(2)}) collective-permute-start(bf16[2,48]{1,0:T(2,128)(2,1)S(1)} %pad_maximum_fusion.38), channel_id=1, source_target_pairs={{0,8},{8,16},{16,24},{24,32},{32,40},{40,48},{48,56},{56,64},{64,7... | collective-permute-start | bytes 584 | tf_op jit(solution)/shard_map/ppermute | solution.py:32
  555.5 16.4 %collective-permute-start.70 = (bf16[80,48]{1,0:T(8,128)(2,1)S(1)}, bf16[80,48]{1,0:T(8,128)(2,1)S(1)}, u32[]{:S(2)}, u32[]{:S(2)}) collective-permute-start(bf16[80,48]{1,0:T(8,128)(2,1)S(1)} %pad_maximum_fusion.34), channel_id=1, source_target_pairs={{0,24},{8,32},{16,40},{24,48},{32,56},{40,64},{48,72},{56,80},{64,... | collective-permute-start | bytes 23048 | tf_op jit(solution)/shard_map/ppermute | solution.py:32
  557.4 14.5 %collective-permute-start.69 = (bf16[80,48]{1,0:T(8,128)(2,1)S(1)}, bf16[80,48]{1,0:T(8,128)(2,1)S(1)}, u32[]{:S(2)}, u32[]{:S(2)}) collective-permute-start(bf16[80,48]{1,0:T(8,128)(2,1)S(1)} %pad_maximum_fusion.34), channel_id=1, source_target_pairs={{0,496},{8,504},{16,0},{24,8},{32,16},{40,24},{48,32},{56,40},{64,... | collective-permute-start | bytes 23048 | tf_op jit(solution)/shard_map/ppermute | solution.py:32
  560.2 11.8 %collective-permute-start.68 = (bf16[80,48]{1,0:T(8,128)(2,1)S(1)}, bf16[80,48]{1,0:T(8,128)(2,1)S(1)}, u32[]{:S(2)}, u32[]{:S(2)}) collective-permute-start(bf16[80,48]{1,0:T(8,128)(2,1)S(1)} %pad_maximum_fusion.34), channel_id=1, source_target_pairs={{0,16},{8,24},{16,32},{24,40},{32,48},{40,56},{48,64},{56,72},{64,... | collective-permute-start | bytes 23048 | tf_op jit(solution)/shard_map/ppermute | solution.py:32
  564.8 7.2 %collective-permute-start.67 = (bf16[80,48]{1,0:T(8,128)(2,1)S(1)}, bf16[80,48]{1,0:T(8,128)(2,1)S(1)}, u32[]{:S(2)}, u32[]{:S(2)}) collective-permute-start(bf16[80,48]{1,0:T(8,128)(2,1)S(1)} %pad_maximum_fusion.34), channel_id=1, source_target_pairs={{0,504},{8,0},{16,8},{24,16},{32,24},{40,32},{48,40},{56,48},{64,5... | collective-permute-start | bytes 23048 | tf_op jit(solution)/shard_map/ppermute | solution.py:32
  570.0 9.0 %collective-permute-start.66 = (bf16[80,48]{1,0:T(8,128)(2,1)S(1)}, bf16[80,48]{1,0:T(8,128)(2,1)S(1)}, u32[]{:S(2)}, u32[]{:S(2)}) collective-permute-start(bf16[80,48]{1,0:T(8,128)(2,1)S(1)} %pad_maximum_fusion.34), channel_id=1, source_target_pairs={{0,8},{8,16},{16,24},{24,32},{32,40},{40,48},{48,56},{56,64},{64,7... | collective-permute-start | bytes 23048 | tf_op jit(solution)/shard_map/ppermute | solution.py:32
  (17 other events, 167.4 us)
where the time goes:
time: 584 us; the launch traced here: 583 us
  local copies, waits for them, and re-layouts  288 us (49%)
  starting transfers between devices  203 us (35%)
  waiting for transfers between devices  81.7 us (14%)
    gather x2, local copies, waits for them, and re-layouts, regress_window(): lon_w = jnp.take(longitude_weight, col_dist, mode='clip')  265 us
    ppermute x40, starting transfers between devices, shifted(): return lax.ppermute(value, axis, pairs)  124 us
    ppermute x16, starting transfers between devices, with_halo(): lax.ppermute(lax.slice_in_dim(block, 0, width, axis=dim), axis, backward)  60 us
    ppermute x40, waiting for transfers between devices, shifted(): return lax.ppermute(value, axis, pairs)  38.5 us
    ppermute x16, waiting for transfers between devices, with_halo(): lax.ppermute(lax.slice_in_dim(block, 0, width, axis=dim), axis, backward)  24.4 us
    ppermute x16, starting transfers between devices, with_halo(): lax.ppermute(lax.slice_in_dim(block, block.shape[dim] - width, None, axis...  18.8 us
    ppermute x16, waiting for transfers between devices, with_halo(): lax.ppermute(lax.slice_in_dim(block, block.shape[dim] - width, None, axis...  18.8 us
    gather x2, local copies, waits for them, and re-layouts, regress_window(): jnp.take(lat_taper, jnp.abs(band_rows[:, None] - obs_row[None, :]), mode=...  15.5 us
  transfers between devices with their start and end apart: 72, of which 21 were waited for; matrix products, arithmetic and copies ran while one was open for 49% of the time, Pallas kernels for 0%

commit v1 on v0

v1 whole, which is shorter than its diff:
```python
import functools

import jax
import jax.numpy as jnp
from jax import lax
from jax.experimental import pallas as pl
from jax.experimental.pallas import tpu as pltpu
from jax.sharding import PartitionSpec as P

REACH = 3
SUB = 4
MOST = 12
TIMESTEP = 0.5
CORIOLIS_FACTOR = 0.3

MEMBERS = 80
ROWS = 8
COLS = 128
SLOTS = 16
PAIRS = 21
OBS = 256
MESH = pl.DeviceIdType.MESH
F32 = jnp.float32
BF16 = jnp.bfloat16

OFFSETS = [
    (dl, dn)
    for dl in sorted(range(-REACH, REACH + 1), key=lambda d: -abs(d))
    for dn in (-1, 1, 0)
    if (dl, dn) != (0, 0)
] + [(0, 0)]


def lanes_of(x, index):
    return jnp.take_along_axis(x, index, axis=1, mode="promise_in_bounds")


def kernel(
    n_lat,
    n_lon,
    state_hbm,
    still_hbm,
    lat_hbm,
    lon_hbm,
    cell_hbm,
    reach_hbm,
    lreach_hbm,
    batch_hbm,
    value_hbm,
    var_hbm,
    out_hbm,
    state,
    still,
    lat_tab,
    lon_tab,
    cell,
    reach,
    lreach,
    batch,
    value,
    var,
    work,
    ns_send,
    ns_recv,
    ew_send,
    ew_recv,
    lab_send,
    lab_recv,
    obs_send,
    obs_recv,
    loc,
    dev,
    small_sem,
    state_sem,
    out_sem,
    ns_ssem,
    ns_rsem,
    ew_ssem,
    ew_rsem,
    lab_ssem,
    lab_rsem,
    obs_ssem,
    obs_rsem,
):
    li = lax.axis_index("lat")
    lo = lax.axis_index("lon")

    def at(dl, dn):
        return (lax.rem(li + dl + n_lat, n_lat), lax.rem(lo + dn + n_lon, n_lon))

    ins = []
    for i, (src, dst) in enumerate(
        (
            (still_hbm, still),
            (lat_hbm, lat_tab),
            (lon_hbm, lon_tab),
            (cell_hbm, cell),
            (reach_hbm, reach),
            (lreach_hbm, lreach),
            (batch_hbm, batch),
            (value_hbm, value),
            (var_hbm, var),
        )
    ):
        ins.append(pltpu.make_async_copy(src, dst, small_sem.at[i]))
        ins[-1].start()
    fields_in = []
    for f in range(3):
        for r in range(ROWS):
            copy = pltpu.make_async_copy(
                state_hbm.at[f, :, r, :], state.at[f, r], state_sem.at[f, r]
            )
            copy.start()
            fields_in.append(copy)

    barrier = pltpu.get_barrier_semaphore()
    for dl, dn in OFFSETS[:-1]:
        pl.semaphore_signal(barrier, inc=1, device_id=at(dl, dn), device_id_type=MESH)

    tile_lane = lax.broadcasted_iota(jnp.int32, (MEMBERS, COLS), 1)
    row_lane = lax.broadcasted_iota(jnp.int32, (1, COLS), 1)

    for copy in ins:
        copy.wait()

    def as_row(ref, fill):
        x = ref[...].reshape(1, SLOTS)
        return jnp.concatenate([x, jnp.full((1, COLS - SLOTS), fill, x.dtype)], axis=1)

    cell_row = as_row(cell, 0)
    reach_row = as_row(reach, 0).astype(F32)
    lreach_row = as_row(lreach, 0).astype(F32)
    batch_row = as_row(batch, -1)
    value_row = as_row(value, 0.0)
    var_row = as_row(var, 1.0)
    lat_rows = cell_row // (COLS * n_lon) - li * ROWS
    lon_cols = lax.rem(cell_row, COLS * n_lon) - lo * COLS
    lat_rows = jnp.where(row_lane < SLOTS, lat_rows, 0)
    lon_cols = jnp.where(row_lane < SLOTS, lon_cols, 0)

    slot_of = lax.broadcasted_iota(jnp.int32, (SLOTS, COLS), 0)
    picks = []
    for b in range(2):
        live = (batch_row == b).astype(jnp.int32)
        upto = live
        for s in (1, 2, 4, 8):
            upto = upto + jnp.where(row_lane >= s, pltpu.roll(upto, s, 1), 0)
        rank = jnp.where(live == 1, upto - 1, -1)
        picks.append((slot_of == rank).astype(F32).astype(BF16))

    sub8 = lax.broadcasted_iota(jnp.int32, (8, COLS), 0)
    labels = jnp.where(
        sub8 == 0,
        lat_rows.astype(F32),
        jnp.where(
            sub8 == 1,
            lon_cols.astype(F32),
            jnp.where(sub8 == 2, reach_row, jnp.where(sub8 == 3, lreach_row, 0.0)),
        ),
    )
    zeros8 = jnp.zeros((8, COLS), F32)
    zeros_rest = jnp.zeros((COLS - 16, COLS), F32)
    rows_to_lanes = (((1,), (1,)), ((), ()))
    label_tile = 0.0
    for b in range(2):
        spread = jnp.concatenate([labels, zeros8] if b == 0 else [zeros8, labels], axis=0)
        spread = jnp.concatenate([spread, zeros_rest], axis=0).astype(BF16)
        label_tile = label_tile + lax.dot_general(
            picks[b], spread, rows_to_lanes, preferred_element_type=F32
        )
    label_tile = label_tile.astype(BF16)
    lab_send[...] = label_tile
    lab_recv[PAIRS - 1] = label_tile

    def send_to_all(src, land, ssem, rsem):
        for i, (dl, dn) in enumerate(OFFSETS[:-1]):
            pltpu.make_async_remote_copy(
                src_ref=src,
                dst_ref=land.at[OFFSETS.index((-dl, -dn))],
                send_sem=ssem,
                recv_sem=rsem,
                device_id=at(dl, dn),
                device_id_type=MESH,
            ).start()

    def all_of(land, ssem, rsem):
        block = land.at[pl.ds(0, PAIRS - 1)]
        return pltpu.make_async_remote_copy(
            src_ref=block,
            dst_ref=block,
            send_sem=ssem,
            recv_sem=rsem,
            device_id=at(0, 1),
            device_id_type=MESH,
        )

    def coriolis(r):
        row = (li * ROWS + r).astype(F32)
        cor = CORIOLIS_FACTOR * (2.0 * (row + 0.5) / (n_lat * ROWS) - 1.0)
        return TIMESTEP * cor

    def gather_rows(land, adjust):
        pieces = []
        for i in range(PAIRS):
            piece = land[i].astype(F32)[:MOST]
            if adjust:
                dl, dn = OFFSETS[i]
                inside = (li + dl >= 0) & (li + dl < n_lat)
                far = jnp.where(inside, -abs(dl), -100).astype(F32)
                lane = row_lane & 7
                piece = piece + (
                    jnp.where(lane == 0, float(dl * ROWS), 0.0)
                    + jnp.where(lane == 1, float(dn * COLS), 0.0)
                    + jnp.where(lane == 2, far, 0.0)
                    + jnp.where(lane == 3, float(-abs(dn)), 0.0)
                )
            pieces.append(piece)
        pieces.append(jnp.zeros((OBS - PAIRS * MOST, COLS), F32))
        return jnp.concatenate(pieces, axis=0)

    def make_locality(b):
        table = gather_rows(lab_recv, True)
        first = 8 * b
        rows = jnp.broadcast_to(table[:, first : first + 1], (OBS, COLS)).astype(jnp.int32)
        cols = jnp.broadcast_to(table[:, first + 1 : first + 2], (OBS, COLS)).astype(jnp.int32)
        within = (table[:, first + 2 : first + 3] >= 0) & (table[:, first + 3 : first + 4] >= 0)
        within = jnp.broadcast_to(jnp.where(within, 1.0 / (MEMBERS - 1), 0.0), (OBS, COLS))
        lane = lax.broadcasted_iota(jnp.int32, (OBS, COLS), 1)
        away = jnp.abs(lane - cols)
        lon_row = lon_tab[...].reshape(1, 2 * COLS)
        low = jnp.broadcast_to(lon_row[:, :COLS], (OBS, COLS))
        high = jnp.broadcast_to(lon_row[:, COLS:], (OBS, COLS))
        lon_w = jnp.where(
            away < COLS, lanes_of(low, away & (COLS - 1)), lanes_of(high, away & (COLS - 1))
        )
        lon_w = lon_w * within
        lat_row = lat_tab[...].reshape(1, 32)
        lat_row = jnp.concatenate([lat_row, jnp.zeros((1, COLS - 32), F32)], axis=1)
        lat_all = jnp.broadcast_to(lat_row, (OBS, COLS))
        for r in range(ROWS):
            loc[b, r] = lanes_of(lat_all, jnp.abs(rows - r)) * lon_w

    edge = jnp.where(
        tile_lane == 0, 0.5 * TIMESTEP, jnp.where(tile_lane == COLS - 1, -0.5 * TIMESTEP, 0.0)
    )
    north_live = (li > 0).astype(F32)
    south_live = (li < n_lat - 1).astype(F32)
    half = 0.5 * TIMESTEP
    sent = []

    for t in range(SUB):
        if t == 0:
            for copy in fields_in:
                copy.wait()
        for r in range(ROWS):
            work[r] = state[2, r] - coriolis(r) * state[1, r]
        ns_send[t, 0, :MEMBERS] = state[0, 0].astype(BF16)
        ns_send[t, 0, MEMBERS:] = (work[0] - half * state[0, 1]).astype(BF16)
        ns_send[t, 1, :MEMBERS] = state[0, ROWS - 1].astype(BF16)
        ns_send[t, 1, MEMBERS:] = (work[ROWS - 1] + half * state[0, ROWS - 2]).astype(BF16)
        if t == 0:
            pl.semaphore_wait(barrier, PAIRS - 1)
        waits = []
        for side, dl in ((0, -1), (1, 1)):
            copy = pltpu.make_async_remote_copy(
                src_ref=ns_send.at[t, side],
                dst_ref=ns_recv.at[t, side],
                send_sem=ns_ssem.at[t, side],
                recv_sem=ns_rsem.at[t, side],
                device_id=at(dl, 0),
                device_id_type=MESH,
            )
            copy.start()
            waits.append(copy)
        packed = jnp.zeros((MEMBERS, COLS), F32)
        for r in range(ROWS):
            h = state[0, r]
            left = pltpu.roll(h, 1, 1)
            right = pltpu.roll(h, COLS - 1, 1)
            z = state[1, r] + coriolis(r) * state[2, r]
            u = (
                z
                + jnp.where(tile_lane == 0, 0.0, half * left)
                - jnp.where(tile_lane == COLS - 1, 0.0, half * right)
            )
            state[1, r] = u
            mixed = jnp.where(tile_lane == COLS - 2, right, jnp.where(tile_lane == 1, left, u))
            packed = jnp.where((tile_lane >> 2) == r, pltpu.roll(mixed, 4 * r + 2, 1), packed)
        ew_send[t] = packed.astype(BF16)
        for side, dn in ((0, -1), (1, 1)):
            copy = pltpu.make_async_remote_copy(
                src_ref=ew_send.at[t],
                dst_ref=ew_recv.at[t, side],
                send_sem=ew_ssem.at[t, side],
                recv_sem=ew_rsem.at[t, side],
                device_id=at(0, dn),
                device_id_type=MESH,
            )
            copy.start()
            waits.append(copy)
        sent.extend(waits)
        if t == 0:
            send_to_all(lab_send, lab_recv, lab_ssem, lab_rsem)
        for r in range(1, ROWS - 1):
            state[2, r] = work[r] - half * (state[0, r + 1] - state[0, r - 1])
        if t == 1:
            all_of(lab_recv, lab_ssem, lab_rsem).wait_recv()
            make_locality(0)
        if t == 2:
            make_locality(1)
        for copy in waits:
            copy.wait_recv()
        south_h = ns_recv[t, 0, :MEMBERS].astype(F32) * south_live
        north_h = ns_recv[t, 1, :MEMBERS].astype(F32) * north_live
        south_v = (ns_recv[t, 0, MEMBERS:].astype(F32) + half * state[0, ROWS - 1]) * south_live
        north_v = (ns_recv[t, 1, MEMBERS:].astype(F32) - half * state[0, 0]) * north_live
        state[2, 0] = work[0] - half * (state[0, 1] - north_h)
        state[2, ROWS - 1] = work[ROWS - 1] - half * (south_h - state[0, ROWS - 2])
        merged = jnp.where(
            (tile_lane & 2) == 0, ew_recv[t, 1].astype(F32), ew_recv[t, 0].astype(F32)
        )
        for r in range(ROWS):
            h = state[0, r]
            far_h = lanes_of(merged, jnp.where(tile_lane == COLS - 1, 4 * r + 3, 4 * r))
            far_q = lanes_of(merged, jnp.where(tile_lane == COLS - 1, 4 * r + 2, 4 * r + 1))
            u = state[1, r] + edge * far_h
            state[1, r] = u
            far_u = far_q - edge * h
            left = jnp.where(tile_lane == 0, far_u, pltpu.roll(u, 1, 1))
            right = jnp.where(tile_lane == COLS - 1, far_u, pltpu.roll(u, COLS - 1, 1))
            below = south_v if r == ROWS - 1 else state[2, r + 1]
            above = north_v if r == 0 else state[2, r - 1]
            depth = half * still[r : r + 1, :]
            state[0, r] = h - depth * ((right - left) + (below - above))

    pick_lane = jnp.broadcast_to(lon_cols, (MEMBERS, COLS))

    def send_observations(b):
        prior = jnp.zeros((MEMBERS, COLS), F32)
        for r in range(ROWS):
            prior = jnp.where(lat_rows == r, lanes_of(state[0, r], pick_lane), prior)
        mean = jnp.sum(prior, axis=0, keepdims=True) / MEMBERS
        away = prior - mean
        total = jnp.sum(away * away, axis=0, keepdims=True) / (MEMBERS - 1) + var_row
        shift = (value_row - mean) / total
        spread = -1.0 / (jnp.sqrt(total) * (jnp.sqrt(var_row) + jnp.sqrt(total)))
        coefs = jnp.where(sub8 == 0, shift, jnp.where(sub8 == 1, spread, 0.0))
        rows = jnp.concatenate(
            [away, coefs, jnp.zeros((COLS - MEMBERS - 8, COLS), F32)], axis=0
        ).astype(BF16)
        tile = lax.dot_general(picks[b], rows, rows_to_lanes, preferred_element_type=F32)
        tile = tile.astype(BF16)
        obs_send[b] = tile
        obs_recv[b, PAIRS - 1] = tile
        send_to_all(obs_send.at[b], obs_recv.at[b], obs_ssem.at[b], obs_rsem.at[b])

    def make_dev(f):
        for r in range(ROWS):
            x = state[f, r]
            mean = jnp.sum(x, axis=0, keepdims=True) / MEMBERS
            dev[f, :, r * COLS : (r + 1) * COLS] = (x - mean).astype(BF16)

    def receive(b):
        all_of(obs_recv.at[b], obs_ssem.at[b], obs_rsem.at[b]).wait_recv()
        table = gather_rows(obs_recv.at[b], False)
        obs_dev = table.astype(BF16)[:, :MEMBERS]
        weights = table[:, MEMBERS : MEMBERS + 1] + table[:, MEMBERS + 1 : MEMBERS + 2] * table
        weights = weights.astype(BF16).astype(F32)
        weights = jnp.transpose(weights).astype(BF16)[:MEMBERS]
        return obs_dev, weights

    def update(b, f, obs_dev, weights, last):
        for pair in range(ROWS // 2):
            lanes = slice(2 * pair * COLS, 2 * (pair + 1) * COLS)
            cov = jnp.dot(obs_dev, dev[f, :, lanes], preferred_element_type=F32)
            taper = jnp.concatenate([loc[b, 2 * pair], loc[b, 2 * pair + 1]], axis=1)
            gain = (cov * taper).astype(BF16)
            step = jnp.dot(weights, gain, preferred_element_type=F32)
            for i in range(2):
                r = 2 * pair + i
                state[f, r] = state[f, r] + step[:, i * COLS : (i + 1) * COLS]
                if last:
                    copy = pltpu.make_async_copy(
                        state.at[f, r], out_hbm.at[f, :, r, :], out_sem.at[f, r]
                    )
                    copy.start()
                    outs.append(copy)

    outs = []
    send_observations(0)
    for f in range(3):
        make_dev(f)
    obs_dev, weights = receive(0)
    update(0, 0, obs_dev, weights, False)
    send_observations(1)
    for f in (1, 2):
        update(0, f, obs_dev, weights, False)
    for f in range(3):
        make_dev(f)
    obs_dev, weights = receive(1)
    for f in range(3):
        update(1, f, obs_dev, weights, True)

    for copy in sent:
        copy.wait_send()
    all_of(lab_recv, lab_ssem, lab_rsem).wait_send()
    for b in range(2):
        all_of(obs_recv.at[b], obs_ssem.at[b], obs_rsem.at[b]).wait_send()
    for copy in outs:
        copy.wait()


def per_device(n_lat, n_lon, *args):
    any_space = pl.BlockSpec(memory_space=pl.ANY)
    vmem = pltpu.VMEM
    dma = pltpu.SemaphoreType.DMA
    ints = vmem((SLOTS,), jnp.int32)
    floats = vmem((SLOTS,), F32)
    return pl.pallas_call(
        functools.partial(kernel, n_lat, n_lon),
        out_shape=jax.ShapeDtypeStruct(args[0].shape, F32),
        in_specs=[any_space] * len(args),
        out_specs=any_space,
        scratch_shapes=[
            vmem((3, ROWS, MEMBERS, COLS), F32),
            vmem((ROWS, COLS), F32),
            vmem((32,), F32),
            vmem((256,), F32),
            ints,
            ints,
            ints,
            ints,
            floats,
            floats,
            vmem((ROWS, MEMBERS, COLS), F32),
            vmem((SUB, 2, 2 * MEMBERS, COLS), BF16),
            vmem((SUB, 2, 2 * MEMBERS, COLS), BF16),
            vmem((SUB, MEMBERS, COLS), BF16),
            vmem((SUB, 2, MEMBERS, COLS), BF16),
            vmem((SLOTS, COLS), BF16),
            vmem((PAIRS, SLOTS, COLS), BF16),
            vmem((2, SLOTS, COLS), BF16),
            vmem((2, PAIRS, SLOTS, COLS), BF16),
            vmem((2, ROWS, OBS, COLS), F32),
            vmem((3, MEMBERS, ROWS * COLS), BF16),
            dma((9,)),
            dma((3, ROWS)),
            dma((3, ROWS)),
            dma((SUB, 2)),
            dma((SUB, 2)),
            dma((SUB, 2)),
            dma((SUB, 2)),
            dma,
            dma,
            dma((2,)),
            dma((2,)),
        ],
        compiler_params=pltpu.CompilerParams(
            collective_id=0, has_side_effects=True, vmem_limit_bytes=32 * 1024 * 1024
        ),
        name="window",
    )(*args)


def solution(mesh):
    return jax.shard_map(
        functools.partial(per_device, mesh.shape["lat"], mesh.shape["lon"]),
        mesh=mesh,
        in_specs=(
            P(None, None, "lat", "lon"),
            P("lat", "lon"),
            P(),
            P(),
            P(("lat", "lon")),
            P(("lat", "lon")),
            P(("lat", "lon")),
            P(("lat", "lon")),
            P(("lat", "lon")),
            P(("lat", "lon")),
        ),
        out_specs=P(None, None, "lat", "lon"),
        check_vma=False,
    )
```

time: 584 us -> 62.2 us (0.11)
  the two profiles are of different devices: /device:TPU:384 before, /device:TPU:1 now
where the time goes in v1:
time: 62.2 us; the launch traced here: 61.9 us
  Pallas kernels  53.8 us (86%)
  local copies, waits for them, and re-layouts  8.1 us (13%)
    pallas_call x1, Pallas kernels, per_device(): pl.pallas_call(functools.partial(kernel, n_lat, n_lon), out_shape=jax.Sha...  53.8 us
    unnamed x21, local copies, waits for them, and re-layouts  8.1 us

profile of v1, /device:TPU:1, one launch (start us, length us, event | category | flops | bytes accessed | tf_op | source)
XLA Modules:
  0.0 61.9 jit_solution(12295285848564711610)
XLA Ops:
  0.0 0.0 copy-start
  0.0 1.2 %copy-done = f32[3,80,8,128]{3,2,1,0:T(8,128)S(1)} copy-done((f32[3,80,8,128]{3,2,1,0:T(8,128)S(1)}, f32[3,80,8,128]{3,2,1,0:T(8,128)}, u32[]{:S(2)}) %copy-start) | copy-done | bytes 983064
  1.2 0.0 copy-start.1
  1.2 0.7 %copy-done.1 = f32[8,128]{1,0:T(8,128)S(1)} copy-done((f32[8,128]{1,0:T(8,128)S(1)}, f32[8,128]{1,0:T(8,128)}, u32[]{:S(2)}) %copy-start.1) | copy-done | bytes 4120
  1.9 0.0 copy-start.2
  1.9 0.7 %copy-done.2 = f32[256]{0:T(256)S(1)} copy-done((f32[256]{0:T(256)S(1)}, f32[256]{0:T(256)}, u32[]{:S(2)}) %copy-start.2) | copy-done | bytes 1048
  2.6 0.0 copy-start.3
  2.6 0.7 %copy-done.3 = f32[32]{0:T(128)S(1)} copy-done((f32[32]{0:T(128)S(1)}, f32[32]{0:T(128)}, u32[]{:S(2)}) %copy-start.3) | copy-done | bytes 152
  3.2 0.0 copy-start.4
  3.2 0.7 %copy-done.4 = s32[16]{0:T(128)S(1)} copy-done((s32[16]{0:T(128)S(1)}, s32[16]{0:T(128)}, u32[]{:S(2)}) %copy-start.4) | copy-done | bytes 88
  3.9 0.0 copy-start.5
  3.9 0.7 %copy-done.5 = s32[16]{0:T(128)S(1)} copy-done((s32[16]{0:T(128)S(1)}, s32[16]{0:T(128)}, u32[]{:S(2)}) %copy-start.5) | copy-done | bytes 88
  4.5 0.0 copy-start.6
  4.5 0.7 %copy-done.6 = s32[16]{0:T(128)S(1)} copy-done((s32[16]{0:T(128)S(1)}, s32[16]{0:T(128)}, u32[]{:S(2)}) %copy-start.6) | copy-done | bytes 88
  5.2 0.0 copy-start.7
  5.2 0.7 %copy-done.7 = s32[16]{0:T(128)S(1)} copy-done((s32[16]{0:T(128)S(1)}, s32[16]{0:T(128)}, u32[]{:S(2)}) %copy-start.7) | copy-done | bytes 88
  5.8 0.0 copy-start.8
  5.9 0.7 %copy-done.8 = f32[16]{0:T(128)S(1)} copy-done((f32[16]{0:T(128)S(1)}, f32[16]{0:T(128)}, u32[]{:S(2)}) %copy-start.8) | copy-done | bytes 88
  6.5 0.0 copy-start.9
  6.5 0.7 %copy-done.9 = f32[16]{0:T(128)S(1)} copy-done((f32[16]{0:T(128)S(1)}, f32[16]{0:T(128)}, u32[]{:S(2)}) %copy-start.9) | copy-done | bytes 88
  7.2 53.8 %window.1 = f32[3,80,8,128]{3,2,1,0:T(8,128)S(1)} custom-call(f32[3,80,8,128]{3,2,1,0:T(8,128)S(1)} %copy-done, f32[8,128]{1,0:T(8,128)S(1)} %copy-done.1, f32[32]{0:T(128)S(1)} %copy-done.3, f32[256]{0:T(256)S(1)} %copy-done.2, s32[16]{0:T(128)S(1)} %copy-done.4, s32[16]{0:T(128)S(1)} %copy-done.5, s32[16]{0:T(128)S(1)} %copy-done.6, s32[16]{0:T(128)S(1)} %copy-done.7, ...), custom_call_target="tpu_custom_call" | custom-call | tf_op jit(solution)/shard_map/window/pallas_call | solution.py:419
  61.0 0.9 %copy.12 = f32[3,80,8,128]{3,2,1,0:T(8,128)} copy(f32[3,80,8,128]{3,2,1,0:T(8,128)S(1)} %window.1) | data formatting | bytes 1966080
Async XLA Ops:
  0.0 1.2 %copy-start = (f32[3,80,8,128]{3,2,1,0:T(8,128)S(1)}, f32[3,80,8,128]{3,2,1,0:T(8,128)}, u32[]{:S(2)}) copy-start(f32[3,80,8,128]{3,2,1,0:T(8,128)} %state_hbm.1) | copy-start | bytes 2949124
  1.2 0.7 %copy-start.1 = (f32[8,128]{1,0:T(8,128)S(1)}, f32[8,128]{1,0:T(8,128)}, u32[]{:S(2)}) copy-start(f32[8,128]{1,0:T(8,128)} %still_hbm.1) | copy-start | bytes 12292
  1.9 0.7 %copy-start.2 = (f32[256]{0:T(256)S(1)}, f32[256]{0:T(256)}, u32[]{:S(2)}) copy-start(f32[256]{0:T(256)} %lon_hbm.1) | copy-start | bytes 3076
  2.6 0.7 %copy-start.3 = (f32[32]{0:T(128)S(1)}, f32[32]{0:T(128)}, u32[]{:S(2)}) copy-start(f32[32]{0:T(128)} %lat_hbm.1) | copy-start | bytes 388
  3.2 0.7 %copy-start.4 = (s32[16]{0:T(128)S(1)}, s32[16]{0:T(128)}, u32[]{:S(2)}) copy-start(s32[16]{0:T(128)} %cell_hbm.1) | copy-start | bytes 196
  3.9 0.7 %copy-start.5 = (s32[16]{0:T(128)S(1)}, s32[16]{0:T(128)}, u32[]{:S(2)}) copy-start(s32[16]{0:T(128)} %reach_hbm.1) | copy-start | bytes 196
  4.5 0.7 %copy-start.6 = (s32[16]{0:T(128)S(1)}, s32[16]{0:T(128)}, u32[]{:S(2)}) copy-start(s32[16]{0:T(128)} %lreach_hbm.1) | copy-start | bytes 196
  5.2 0.7 %copy-start.7 = (s32[16]{0:T(128)S(1)}, s32[16]{0:T(128)}, u32[]{:S(2)}) copy-start(s32[16]{0:T(128)} %batch_hbm.1) | copy-start | bytes 196
  5.8 0.7 %copy-start.8 = (f32[16]{0:T(128)S(1)}, f32[16]{0:T(128)}, u32[]{:S(2)}) copy-start(f32[16]{0:T(128)} %value_hbm.1) | copy-start | bytes 196
  6.5 0.7 %copy-start.9 = (f32[16]{0:T(128)S(1)}, f32[16]{0:T(128)}, u32[]{:S(2)}) copy-start(f32[16]{0:T(128)} %var_hbm.1) | copy-start | bytes 196

commit v2 on v1

--- a/solution.py
+++ b/solution.py
@@ -23,12 +23,9 @@
 F32 = jnp.float32
 BF16 = jnp.bfloat16
 
-OFFSETS = [
-    (dl, dn)
-    for dl in sorted(range(-REACH, REACH + 1), key=lambda d: -abs(d))
-    for dn in (-1, 1, 0)
-    if (dl, dn) != (0, 0)
-] + [(0, 0)]
+BANDS = (-3, 3, -2, 2, -1, 1, 0)
+SECTORS = (-1, 1, 0)
+OFFSETS = [(dl, dn) for dl in BANDS for dn in SECTORS]
 
 
 def lanes_of(x, index):
@@ -48,7 +45,7 @@
     batch_hbm,
     value_hbm,
     var_hbm,
-    out_hbm,
+    out,
     state,
     still,
     lat_tab,
@@ -72,7 +69,6 @@
     dev,
     small_sem,
     state_sem,
-    out_sem,
     ns_ssem,
     ns_rsem,
     ew_ssem,
@@ -86,7 +82,17 @@
     lo = lax.axis_index("lon")
 
     def at(dl, dn):
-        return (lax.rem(li + dl + n_lat, n_lat), lax.rem(lo + dn + n_lon, n_lon))
+        return (li + dl, lax.rem(lo + dn + n_lon, n_lon))
+
+    def if_band(dl, act):
+        if dl == 0:
+            act()
+        else:
+            pl.when((li + dl >= 0) & (li + dl < n_lat))(act)
+
+    def unless_band(dl, act):
+        if dl != 0:
+            pl.when((li + dl < 0) | (li + dl >= n_lat))(act)
 
     ins = []
     for i, (src, dst) in enumerate(
@@ -114,8 +120,36 @@
             fields_in.append(copy)
 
     barrier = pltpu.get_barrier_semaphore()
-    for dl, dn in OFFSETS[:-1]:
-        pl.semaphore_signal(barrier, inc=1, device_id=at(dl, dn), device_id_type=MESH)
+    for dl in BANDS:
+
+        def greet(dl=dl):
+            for dn in SECTORS:
+                if (dl, dn) != (0, 0):
+                    pl.semaphore_signal(barrier, inc=1, device_id=at(dl, dn), device_id_type=MESH)
+
+        if_band(dl, greet)
+
+    def met_all():
+        def meet(bands):
+            pl.semaphore_wait(barrier, 2 + 3 * bands)
+
+        for k in range(REACH):
+            pl.when(li == k)(lambda k=k: meet(REACH + k))
+            pl.when(li == n_lat - 1 - k)(lambda k=k: meet(REACH + k))
+        pl.when((li >= REACH) & (li < n_lat - REACH))(lambda: meet(2 * REACH))
+
+    for g, dl in enumerate(BANDS):
+
+        def clear(g=g, dl=dl):
+            group = pl.ds(3 * g, 3)
+            lab_recv[group] = jnp.zeros((3, SLOTS, COLS), BF16)
+            for b in range(2):
+                obs_recv[b, group] = jnp.zeros((3, SLOTS, COLS), BF16)
+            if abs(dl) == 1:
+                for t in range(SUB):
+                    ns_recv[t, (1 - dl) // 2] = jnp.zeros((2 * MEMBERS, COLS), BF16)
+
+        unless_band(dl, clear)
 
     tile_lane = lax.broadcasted_iota(jnp.int32, (MEMBERS, COLS), 1)
     row_lane = lax.broadcasted_iota(jnp.int32, (1, COLS), 1)
@@ -173,26 +207,45 @@
     lab_recv[PAIRS - 1] = label_tile
 
     def send_to_all(src, land, ssem, rsem):
-        for i, (dl, dn) in enumerate(OFFSETS[:-1]):
-            pltpu.make_async_remote_copy(
-                src_ref=src,
-                dst_ref=land.at[OFFSETS.index((-dl, -dn))],
-                send_sem=ssem,
-                recv_sem=rsem,
-                device_id=at(dl, dn),
-                device_id_type=MESH,
-            ).start()
-
-    def all_of(land, ssem, rsem):
-        block = land.at[pl.ds(0, PAIRS - 1)]
-        return pltpu.make_async_remote_copy(
-            src_ref=block,
-            dst_ref=block,
-            send_sem=ssem,
-            recv_sem=rsem,
-            device_id=at(0, 1),
-            device_id_type=MESH,
-        )
+        for g, dl in enumerate(BANDS):
+
+            def send(g=g, dl=dl):
+                for dn in SECTORS:
+                    if (dl, dn) != (0, 0):
+                        pltpu.make_async_remote_copy(
+                            src_ref=src,
+                            dst_ref=land.at[OFFSETS.index((-dl, -dn))],
+                            send_sem=ssem.at[g],
+                            recv_sem=rsem.at[BANDS.index(-dl)],
+                            device_id=at(dl, dn),
+                            device_id_type=MESH,
+                        ).start()
+
+            if_band(dl, send)
+
+    def for_all(land, ssem, rsem, act):
+        for g, dl in enumerate(BANDS):
+
+            def wait(g=g, dl=dl):
+                block = land.at[pl.ds(3 * g, 2 if dl == 0 else 3)]
+                act(
+                    pltpu.make_async_remote_copy(
+                        src_ref=block,
+                        dst_ref=block,
+                        send_sem=ssem.at[g],
+                        recv_sem=rsem.at[g],
+                        device_id=at(0, 1),
+                        device_id_type=MESH,
+                    )
+                )
+
+            if_band(dl, wait)
+
+    def all_received(*refs):
+        for_all(*refs, lambda copy: copy.wait_recv())
+
+    def all_sent(*refs):
+        for_all(*refs, lambda copy: copy.wait_send())
 
     def coriolis(r):
         row = (li * ROWS + r).astype(F32)
@@ -259,8 +312,8 @@
         ns_send[t, 1, :MEMBERS] = state[0, ROWS - 1].astype(BF16)
         ns_send[t, 1, MEMBERS:] = (work[ROWS - 1] + half * state[0, ROWS - 2]).astype(BF16)
         if t == 0:
-            pl.semaphore_wait(barrier, PAIRS - 1)
-        waits = []
+            met_all()
+        copies = []
         for side, dl in ((0, -1), (1, 1)):
             copy = pltpu.make_async_remote_copy(
                 src_ref=ns_send.at[t, side],
@@ -270,8 +323,8 @@
                 device_id=at(dl, 0),
                 device_id_type=MESH,
             )
-            copy.start()
-            waits.append(copy)
+            if_band(dl, copy.start)
+            copies.append((copy, dl, -dl))
         packed = jnp.zeros((MEMBERS, COLS), F32)
         for r in range(ROWS):
             h = state[0, r]
@@ -297,19 +350,19 @@
                 device_id_type=MESH,
             )
             copy.start()
-            waits.append(copy)
-        sent.extend(waits)
+            copies.append((copy, 0, 0))
+        sent.extend(copies)
         if t == 0:
             send_to_all(lab_send, lab_recv, lab_ssem, lab_rsem)
         for r in range(1, ROWS - 1):
             state[2, r] = work[r] - half * (state[0, r + 1] - state[0, r - 1])
         if t == 1:
-            all_of(lab_recv, lab_ssem, lab_rsem).wait_recv()
+            all_received(lab_recv, lab_ssem, lab_rsem)
             make_locality(0)
         if t == 2:
             make_locality(1)
-        for copy in waits:
-            copy.wait_recv()
+        for copy, _, dl in copies:
+            if_band(dl, copy.wait_recv)
         south_h = ns_recv[t, 0, :MEMBERS].astype(F32) * south_live
         north_h = ns_recv[t, 1, :MEMBERS].astype(F32) * north_live
         south_v = (ns_recv[t, 0, MEMBERS:].astype(F32) + half * state[0, ROWS - 1]) * south_live
@@ -361,7 +414,7 @@
             dev[f, :, r * COLS : (r + 1) * COLS] = (x - mean).astype(BF16)
 
     def receive(b):
-        all_of(obs_recv.at[b], obs_ssem.at[b], obs_rsem.at[b]).wait_recv()
+        all_received(obs_recv.at[b], obs_ssem.at[b], obs_rsem.at[b])
         table = gather_rows(obs_recv.at[b], False)
         obs_dev = table.astype(BF16)[:, :MEMBERS]
         weights = table[:, MEMBERS : MEMBERS + 1] + table[:, MEMBERS + 1 : MEMBERS + 2] * table
@@ -378,15 +431,12 @@
             step = jnp.dot(weights, gain, preferred_element_type=F32)
             for i in range(2):
                 r = 2 * pair + i
-                state[f, r] = state[f, r] + step[:, i * COLS : (i + 1) * COLS]
+                new = state[f, r] + step[:, i * COLS : (i + 1) * COLS]
                 if last:
-                    copy = pltpu.make_async_copy(
-                        state.at[f, r], out_hbm.at[f, :, r, :], out_sem.at[f, r]
-                    )
-                    copy.start()
-                    outs.append(copy)
-
-    outs = []
+                    out[f, :, r, :] = new
+                else:
+                    state[f, r] = new
+
     send_observations(0)
     for f in range(3):
         make_dev(f)
@@ -401,26 +451,24 @@
     for f in range(3):
         update(1, f, obs_dev, weights, True)
 
-    for copy in sent:
-        copy.wait_send()
-    all_of(lab_recv, lab_ssem, lab_rsem).wait_send()
+    for copy, dl, _ in sent:
+        if_band(dl, copy.wait_send)
+    all_sent(lab_recv, lab_ssem, lab_rsem)
     for b in range(2):
-        all_of(obs_recv.at[b], obs_ssem.at[b], obs_rsem.at[b]).wait_send()
-    for copy in outs:
-        copy.wait()
+        all_sent(obs_recv.at[b], obs_ssem.at[b], obs_rsem.at[b])
 
 
 def per_device(n_lat, n_lon, *args):
-    any_space = pl.BlockSpec(memory_space=pl.ANY)
+    args = [pltpu.with_memory_space_constraint(arg, pltpu.HBM) for arg in args]
     vmem = pltpu.VMEM
     dma = pltpu.SemaphoreType.DMA
     ints = vmem((SLOTS,), jnp.int32)
     floats = vmem((SLOTS,), F32)
     return pl.pallas_call(
         functools.partial(kernel, n_lat, n_lon),
-        out_shape=jax.ShapeDtypeStruct(args[0].shape, F32),
-        in_specs=[any_space] * len(args),
-        out_specs=any_space,
+        out_shape=vmem(args[0].shape, F32),
+        in_specs=[pl.BlockSpec(memory_space=pltpu.HBM)] * len(args),
+        out_specs=pl.BlockSpec(memory_space=vmem),
         scratch_shapes=[
             vmem((3, ROWS, MEMBERS, COLS), F32),
             vmem((ROWS, COLS), F32),
@@ -445,18 +493,17 @@
             vmem((3, MEMBERS, ROWS * COLS), BF16),
             dma((9,)),
             dma((3, ROWS)),
-            dma((3, ROWS)),
             dma((SUB, 2)),
             dma((SUB, 2)),
             dma((SUB, 2)),
             dma((SUB, 2)),
-            dma,
-            dma,
-            dma((2,)),
-            dma((2,)),
+            dma((len(BANDS),)),
+            dma((len(BANDS),)),
+            dma((2, len(BANDS))),
+            dma((2, len(BANDS))),
         ],
         compiler_params=pltpu.CompilerParams(
-            collective_id=0, has_side_effects=True, vmem_limit_bytes=32 * 1024 * 1024
+            collective_id=0, has_side_effects=True, vmem_limit_bytes=60 * 1024 * 1024
         ),
         name="window",
     )(*args)

time: 62.2 us -> 45.3 us (0.73)
  the two profiles are of different devices: /device:TPU:1 before, /device:TPU:384 now
where the time goes in v2:
time: 45.3 us; the launch traced here: 45.1 us
  Pallas kernels  44.2 us (98%)
  local copies, waits for them, and re-layouts  0.95 us (2%)
    pallas_call x1, Pallas kernels, per_device(): pl.pallas_call(functools.partial(kernel, n_lat, n_lon), out_shape=vmem(ar...  44.2 us
    unnamed x1, local copies, waits for them, and re-layouts  0.95 us

profile of v2, /device:TPU:384, one launch (start us, length us, event | category | flops | bytes accessed | tf_op | source)
XLA Modules:
  0.0 45.1 jit_solution(13668718120087036450)
XLA Ops:
  0.0 44.2 %window.1 = f32[3,80,8,128]{3,2,1,0:T(8,128)S(1)} custom-call(f32[3,80,8,128]{3,2,1,0:T(8,128)} %state_hbm.1, f32[8,128]{1,0:T(8,128)} %still_hbm.1, f32[32]{0:T(128)} %lat_hbm.1, f32[256]{0:T(256)} %lon_hbm.1, s32[16]{0:T(128)} %cell_hbm.1, s32[16]{0:T(128)} %reach_hbm.1, s32[16]{0:T(128)} %lreach_hbm.1, s32[16]{0:T(128)} %batch_hbm.1, f32[16]{0:T(128)} %value_hbm.1, ...), custom_call_target="tpu_custom_call" | custom-call | tf_op jit(solution)/shard_map/window/pallas_call | solution.py:467
  44.2 0.9 %copy.12 = f32[3,80,8,128]{3,2,1,0:T(8,128)} copy(f32[3,80,8,128]{3,2,1,0:T(8,128)S(1)} %window.1) | data formatting | bytes 1966080

commit v3 on v2

--- a/solution.py
+++ b/solution.py
@@ -26,6 +26,7 @@
 BANDS = (-3, 3, -2, 2, -1, 1, 0)
 SECTORS = (-1, 1, 0)
 OFFSETS = [(dl, dn) for dl in BANDS for dn in SECTORS]
+SIDES = [(0, -1), (0, 1), (-1, -1), (-1, 1), (1, -1), (1, 1)]
 
 
 def lanes_of(x, index):
@@ -57,6 +58,7 @@
     value,
     var,
     work,
+    outside,
     ns_send,
     ns_recv,
     ew_send,
@@ -146,8 +148,10 @@
             for b in range(2):
                 obs_recv[b, group] = jnp.zeros((3, SLOTS, COLS), BF16)
             if abs(dl) == 1:
-                for t in range(SUB):
-                    ns_recv[t, (1 - dl) // 2] = jnp.zeros((2 * MEMBERS, COLS), BF16)
+                for t in range(SUB // 2):
+                    ns_recv[t, (1 - dl) // 2] = jnp.zeros(ns_recv.shape[2:], BF16)
+                    for dn in (-1, 1):
+                        ew_recv[t, SIDES.index((-dl, dn))] = jnp.zeros(ew_recv.shape[2:], BF16)
 
         unless_band(dl, clear)
 
@@ -293,31 +297,95 @@
         for r in range(ROWS):
             loc[b, r] = lanes_of(lat_all, jnp.abs(rows - r)) * lon_w
 
-    edge = jnp.where(
-        tile_lane == 0, 0.5 * TIMESTEP, jnp.where(tile_lane == COLS - 1, -0.5 * TIMESTEP, 0.0)
+    first = tile_lane == 0
+    final = tile_lane == COLS - 1
+    half = 0.5 * TIMESTEP
+    edge = jnp.where(first, half, jnp.where(final, -half, 0.0))
+    corner = jnp.where(
+        first,
+        1.0,
+        jnp.where(final, -1.0, jnp.where((tile_lane == 1) | (tile_lane == COLS - 2), half, 0.0)),
     )
     north_live = (li > 0).astype(F32)
     south_live = (li < n_lat - 1).astype(F32)
-    half = 0.5 * TIMESTEP
     sent = []
-
-    for t in range(SUB):
+    bottom = ROWS - 1
+
+    def rolled(x, steps):
+        return pltpu.roll(x, steps % COLS, 1)
+
+    def depth(r):
+        return half * still[r : r + 1, :]
+
+    def apart(u, outside):
+        left = jnp.where(first, outside, rolled(u, 1))
+        right = jnp.where(final, outside, rolled(u, -1))
+        return right - left
+
+    def at_ends(x, a, b):
+        return lanes_of(x, jnp.where(final, b, a))
+
+    def at_four(x, a, b, c, d):
+        near = jnp.where(tile_lane == 1, b, a)
+        return lanes_of(x, jnp.where(final, d, jnp.where(tile_lane == COLS - 2, c, near)))
+
+    def put(packed, place, x):
+        return jnp.where((tile_lane >> 2) == place, rolled(x, 4 * place + 2), packed)
+
+    def middle(ends, second_last, second):
+        return jnp.where(
+            tile_lane == COLS - 2, second_last, jnp.where(tile_lane == 1, second, ends)
+        )
+
+    for t in range(SUB // 2):
         if t == 0:
             for copy in fields_in:
                 copy.wait()
-        for r in range(ROWS):
-            work[r] = state[2, r] - coriolis(r) * state[1, r]
-        ns_send[t, 0, :MEMBERS] = state[0, 0].astype(BF16)
-        ns_send[t, 0, MEMBERS:] = (work[0] - half * state[0, 1]).astype(BF16)
-        ns_send[t, 1, :MEMBERS] = state[0, ROWS - 1].astype(BF16)
-        ns_send[t, 1, MEMBERS:] = (work[ROWS - 1] + half * state[0, ROWS - 2]).astype(BF16)
+        packed = jnp.zeros((MEMBERS, COLS), F32)
+
+        def velocities(r, packed):
+            h, u, v = state[0, r], state[1, r], state[2, r]
+            left, right = rolled(h, 1), rolled(h, -1)
+            turn = coriolis(r)
+            new_u = u + turn * v + jnp.where(first, 0.0, half * left)
+            new_u = new_u - jnp.where(final, 0.0, half * right)
+            new_v = v - turn * u
+            if r > 0:
+                new_v = new_v + half * state[0, r - 1]
+            if r < bottom:
+                new_v = new_v - half * state[0, r + 1]
+            state[1, r] = new_u
+            state[2, r] = new_v
+            return put(packed, r, middle(new_u, right, left))
+
+        def heights(r):
+            h = state[0, r]
+            above = state[2, r - 1] if r > 0 else -half * north_live * h
+            below = state[2, r + 1] if r < bottom else half * south_live * h
+            around = apart(state[1, r], -edge * h) + (below - above)
+            work[r] = h - depth(r) * around
+
+        for r in (0, 1, 2, 7, 6, 5):
+            packed = velocities(r, packed)
+        for r in (0, 1, 7, 6):
+            heights(r)
+        for side, outer, inner, sign in ((0, 0, 1, -half), (1, bottom, bottom - 1, half)):
+            second = state[2, outer] - coriolis(outer) * state[1, outer] + sign * work[inner]
+            for i, x in enumerate((state[0, outer], state[2, outer], work[outer], second)):
+                ns_send[t, side, i * MEMBERS : (i + 1) * MEMBERS] = x.astype(BF16)
+            if t == 0:
+                rows = jnp.concatenate(
+                    [depth(outer), depth(inner), jnp.zeros((14, COLS), F32)], axis=0
+                )
+                ns_send[t, side, 4 * MEMBERS :] = rows.astype(BF16)
         if t == 0:
             met_all()
         copies = []
         for side, dl in ((0, -1), (1, 1)):
+            rows = pl.ds(0, 4 * MEMBERS + (16 if t == 0 else 0))
             copy = pltpu.make_async_remote_copy(
-                src_ref=ns_send.at[t, side],
-                dst_ref=ns_recv.at[t, side],
+                src_ref=ns_send.at[t, side, rows],
+                dst_ref=ns_recv.at[t, side, rows],
                 send_sem=ns_ssem.at[t, side],
                 recv_sem=ns_rsem.at[t, side],
                 device_id=at(dl, 0),
@@ -325,66 +393,142 @@
             )
             if_band(dl, copy.start)
             copies.append((copy, dl, -dl))
-        packed = jnp.zeros((MEMBERS, COLS), F32)
-        for r in range(ROWS):
-            h = state[0, r]
-            left = pltpu.roll(h, 1, 1)
-            right = pltpu.roll(h, COLS - 1, 1)
-            z = state[1, r] + coriolis(r) * state[2, r]
-            u = (
-                z
-                + jnp.where(tile_lane == 0, 0.0, half * left)
-                - jnp.where(tile_lane == COLS - 1, 0.0, half * right)
-            )
-            state[1, r] = u
-            mixed = jnp.where(tile_lane == COLS - 2, right, jnp.where(tile_lane == 1, left, u))
-            packed = jnp.where((tile_lane >> 2) == r, pltpu.roll(mixed, 4 * r + 2, 1), packed)
-        ew_send[t] = packed.astype(BF16)
-        for side, dn in ((0, -1), (1, 1)):
+        for r in (3, 4):
+            packed = velocities(r, packed)
+        for r in (2, 3, 4, 5):
+            heights(r)
+        for r in range(ROWS):
+            h = work[r]
+            left, right = rolled(h, 1), rolled(h, -1)
+            second = state[1, r] + coriolis(r) * state[2, r]
+            second = second + jnp.where(final, half * left, -half * right)
+            packed = put(packed, ROWS + r, middle(second, right, left))
+        for i, x in enumerate((state[2, 0], state[2, bottom], state[0, 0], state[0, bottom])):
+            packed = put(packed, 2 * ROWS + i, x)
+        ew_send[t, :MEMBERS] = packed.astype(BF16)
+        if t == 0:
+            rows = jnp.concatenate([half * still[...], zeros8], axis=0)
+            ew_send[t, MEMBERS:] = rows.astype(BF16)
+        for i, (dl, dn) in enumerate(SIDES):
+            rows = pl.ds(0, MEMBERS + (16 if t == 0 else 0))
             copy = pltpu.make_async_remote_copy(
-                src_ref=ew_send.at[t],
-                dst_ref=ew_recv.at[t, side],
-                send_sem=ew_ssem.at[t, side],
-                recv_sem=ew_rsem.at[t, side],
-                device_id=at(0, dn),
+                src_ref=ew_send.at[t, rows],
+                dst_ref=ew_recv.at[t, i, rows],
+                send_sem=ew_ssem.at[t, i],
+                recv_sem=ew_rsem.at[t, i],
+                device_id=at(dl, dn),
                 device_id_type=MESH,
             )
-            copy.start()
-            copies.append((copy, 0, 0))
+            if_band(dl, copy.start)
+            copies.append((copy, dl, -dl))
         sent.extend(copies)
         if t == 0:
             send_to_all(lab_send, lab_recv, lab_ssem, lab_rsem)
-        for r in range(1, ROWS - 1):
-            state[2, r] = work[r] - half * (state[0, r + 1] - state[0, r - 1])
         if t == 1:
             all_received(lab_recv, lab_ssem, lab_rsem)
             make_locality(0)
-        if t == 2:
-            make_locality(1)
         for copy, _, dl in copies:
             if_band(dl, copy.wait_recv)
-        south_h = ns_recv[t, 0, :MEMBERS].astype(F32) * south_live
-        north_h = ns_recv[t, 1, :MEMBERS].astype(F32) * north_live
-        south_v = (ns_recv[t, 0, MEMBERS:].astype(F32) + half * state[0, ROWS - 1]) * south_live
-        north_v = (ns_recv[t, 1, MEMBERS:].astype(F32) - half * state[0, 0]) * north_live
-        state[2, 0] = work[0] - half * (state[0, 1] - north_h)
-        state[2, ROWS - 1] = work[ROWS - 1] - half * (south_h - state[0, ROWS - 2])
-        merged = jnp.where(
-            (tile_lane & 2) == 0, ew_recv[t, 1].astype(F32), ew_recv[t, 0].astype(F32)
+
+        def from_ends(dl):
+            west = ew_recv[t, SIDES.index((-dl, 1)), :MEMBERS].astype(F32)
+            east = ew_recv[t, SIDES.index((-dl, -1)), :MEMBERS].astype(F32)
+            return jnp.where((tile_lane & 2) == 0, west, east)
+
+        def from_rows(side):
+            x = [ns_recv[t, side, i * MEMBERS : (i + 1) * MEMBERS].astype(F32) for i in range(4)]
+            rows = ns_recv[0, side, 4 * MEMBERS :].astype(F32)
+            return x + [rows[0:1], rows[1:2]]
+
+        south_h, south_v, south_h1, south_v2, south_d1, south_d2 = from_rows(0)
+        north_h, north_v, north_h1, north_v2, north_d1, north_d2 = from_rows(1)
+        ends_d = [
+            ew_recv[0, SIDES.index((0, dn)), MEMBERS:].astype(F32)[:ROWS] for dn in (1, -1)
+        ]
+        end_lane = lax.broadcasted_iota(jnp.int32, (ROWS, COLS), 1)
+        d1, d2 = (
+            jnp.where(
+                end_lane == 0,
+                rolled(ends_d[0], k),
+                jnp.where(end_lane == COLS - 1, rolled(ends_d[1], -k), 0.0),
+            )
+            for k in (1, 2)
         )
+        corners = {}
+        for name, dl, outer, inner, k in (("n", -1, bottom, bottom - 1, 1), ("s", 1, 0, 1, 0)):
+            x = from_ends(dl)
+            v, h = 4 * (2 * ROWS + k), 4 * (2 * ROWS + 2 + k)
+            corners[name] = (
+                at_ends(x, 4 * outer, 4 * outer + 3),
+                at_four(x, 4 * outer + 1, 4 * outer, 4 * outer + 3, 4 * outer + 2),
+                at_four(x, 4 * inner + 1, 4 * inner, 4 * inner + 3, 4 * inner + 2),
+                at_ends(x, v + 1, v + 2),
+                at_ends(x, v, v + 3),
+                at_ends(x, h, h + 3),
+            )
+        n_h, n_row1, n_row2, n_v, n_v_in, n_h_in = corners["n"]
+        s_h, s_row1, s_row2, s_v, s_v_in, s_h_in = corners["s"]
+
+        top, low = state[0, 0], state[0, bottom]
+        top_v = state[2, 0] + half * north_h
+        low_v = state[2, bottom] - half * south_h
+        state[2, 0] = top_v
+        state[2, bottom] = low_v
+        north_v = (north_v - half * top) * north_live
+        south_v = (south_v + half * low) * south_live
+        north_h1 = north_h1 - north_d1 * (top_v - half * north_h) + north_d1 * corner * n_row1
+        south_h1 = south_h1 + south_d1 * (low_v + half * south_h) + south_d1 * corner * s_row1
+        north_h1 = north_h1 * north_live
+        south_h1 = south_h1 * south_live
+        north_v2 = north_v2 - half * top * (1.0 - half * north_d2)
+        north_v2 = north_v2 + half * north_d2 * corner * n_row2 - coriolis(-1) * edge * n_h
+        south_v2 = south_v2 + half * low * (1.0 - half * south_d2)
+        south_v2 = south_v2 - half * south_d2 * corner * s_row2 - coriolis(ROWS) * edge * s_h
+
+        ends = from_ends(0)
         for r in range(ROWS):
             h = state[0, r]
-            far_h = lanes_of(merged, jnp.where(tile_lane == COLS - 1, 4 * r + 3, 4 * r))
-            far_q = lanes_of(merged, jnp.where(tile_lane == COLS - 1, 4 * r + 2, 4 * r + 1))
+            a, b = 4 * r, 4 * (ROWS + r)
+            far_h = at_ends(ends, a, a + 3)
+            far_u = at_ends(ends, a + 1, a + 2)
+            far_h1 = at_ends(ends, b, b + 3)
+            far_u2 = at_ends(ends, b + 1, b + 2)
             u = state[1, r] + edge * far_h
             state[1, r] = u
-            far_u = far_q - edge * h
-            left = jnp.where(tile_lane == 0, far_u, pltpu.roll(u, 1, 1))
-            right = jnp.where(tile_lane == COLS - 1, far_u, pltpu.roll(u, COLS - 1, 1))
-            below = south_v if r == ROWS - 1 else state[2, r + 1]
-            above = north_v if r == 0 else state[2, r - 1]
-            depth = half * still[r : r + 1, :]
-            state[0, r] = h - depth * ((right - left) + (below - above))
+            above = state[2, r - 1] if r > 0 else north_v
+            below = state[2, r + 1] if r < bottom else south_v
+            work[r] = h - depth(r) * (apart(u, far_u - edge * h) + (below - above))
+            end_d1, end_d2 = d1[r : r + 1], d2[r : r + 1]
+            far_h1 = far_h1 - end_d1 * (edge * (1.0 / half) * u - half * far_h)
+            far_u2 = far_u2 - edge * h * (1.0 - half * end_d2)
+            if r == 0:
+                far_h1 = far_h1 + end_d1 * n_v
+                far_u2 = far_u2 + coriolis(r) * half * n_h + edge * end_d2 * n_v_in
+            if r == 1:
+                far_h1 = far_h1 + half * end_d1 * n_h
+                far_u2 = far_u2 + half * edge * end_d2 * n_h_in
+            if r == bottom - 1:
+                far_h1 = far_h1 + half * end_d1 * s_h
+                far_u2 = far_u2 + half * edge * end_d2 * s_h_in
+            if r == bottom:
+                far_h1 = far_h1 - end_d1 * s_v
+                far_u2 = far_u2 - coriolis(r) * half * s_h - edge * end_d2 * s_v_in
+            outside[0, r] = far_h1
+            outside[1, r] = far_u2
+        for r in range(ROWS):
+            h, u, v = work[r], state[1, r], state[2, r]
+            above = work[r - 1] if r > 0 else north_h1
+            below = work[r + 1] if r < bottom else south_h1
+            state[1, r] = u + coriolis(r) * v - half * apart(h, outside[0, r])
+            state[2, r] = v - coriolis(r) * u - half * (below - above)
+        north_v2 = (north_v2 - half * work[0]) * north_live
+        south_v2 = (south_v2 + half * work[bottom]) * south_live
+        for r in range(ROWS):
+            h = work[r]
+            above = state[2, r - 1] if r > 0 else north_v2
+            below = state[2, r + 1] if r < bottom else south_v2
+            around = apart(state[1, r], outside[1, r] - edge * h) + (below - above)
+            state[0, r] = h - depth(r) * around
 
     pick_lane = jnp.broadcast_to(lon_cols, (MEMBERS, COLS))
 
@@ -440,6 +584,7 @@
     send_observations(0)
     for f in range(3):
         make_dev(f)
+    make_locality(1)
     obs_dev, weights = receive(0)
     update(0, 0, obs_dev, weights, False)
     send_observations(1)
@@ -481,10 +626,11 @@
             floats,
             floats,
             vmem((ROWS, MEMBERS, COLS), F32),
-            vmem((SUB, 2, 2 * MEMBERS, COLS), BF16),
-            vmem((SUB, 2, 2 * MEMBERS, COLS), BF16),
-            vmem((SUB, MEMBERS, COLS), BF16),
-            vmem((SUB, 2, MEMBERS, COLS), BF16),
+            vmem((2, ROWS, MEMBERS, COLS), F32),
+            vmem((SUB // 2, 2, 4 * MEMBERS + 16, COLS), BF16),
+            vmem((SUB // 2, 2, 4 * MEMBERS + 16, COLS), BF16),
+            vmem((SUB // 2, MEMBERS + 16, COLS), BF16),
+            vmem((SUB // 2, len(SIDES), MEMBERS + 16, COLS), BF16),
             vmem((SLOTS, COLS), BF16),
             vmem((PAIRS, SLOTS, COLS), BF16),
             vmem((2, SLOTS, COLS), BF16),
@@ -493,10 +639,10 @@
             vmem((3, MEMBERS, ROWS * COLS), BF16),
             dma((9,)),
             dma((3, ROWS)),
-            dma((SUB, 2)),
-            dma((SUB, 2)),
-            dma((SUB, 2)),
-            dma((SUB, 2)),
+            dma((SUB // 2, 2)),
+            dma((SUB // 2, 2)),
+            dma((SUB // 2, len(SIDES))),
+            dma((SUB // 2, len(SIDES))),
             dma((len(BANDS),)),
             dma((len(BANDS),)),
             dma((2, len(BANDS))),

time: 45.3 us -> 40.7 us (0.90)
  Pallas kernels: 44.2 us -> 39.5 us
    pallas_call x1, Pallas kernels: 44.2 us -> 39.5 us  [per_device(): pl.pallas_call(functools.partial(kernel, n_lat, n_lon), out_shape=vmem(ar...]
where the time goes in v3:
time: 40.7 us; the launch traced here: 40.5 us
  Pallas kernels  39.5 us (97%)
  local copies, waits for them, and re-layouts  0.95 us (2%)
    pallas_call x1, Pallas kernels, per_device(): pl.pallas_call(functools.partial(kernel, n_lat, n_lon), out_shape=vmem(ar...  39.5 us
    unnamed x1, local copies, waits for them, and re-layouts  0.95 us

profile of v3, /device:TPU:384, one launch (start us, length us, event | category | flops | bytes accessed | tf_op | source)
XLA Modules:
  0.0 40.5 jit_solution(11880549931845953023)
XLA Ops:
  0.0 39.5 %window.1 = f32[3,80,8,128]{3,2,1,0:T(8,128)S(1)} custom-call(f32[3,80,8,128]{3,2,1,0:T(8,128)} %state_hbm.1, f32[8,128]{1,0:T(8,128)} %still_hbm.1, f32[32]{0:T(128)} %lat_hbm.1, f32[256]{0:T(256)} %lon_hbm.1, s32[16]{0:T(128)} %cell_hbm.1, s32[16]{0:T(128)} %reach_hbm.1, s32[16]{0:T(128)} %lreach_hbm.1, s32[16]{0:T(128)} %batch_hbm.1, f32[16]{0:T(128)} %value_hbm.1, ...), custom_call_target="tpu_custom_call" | custom-call | tf_op jit(solution)/shard_map/window/pallas_call | solution.py:612
  39.5 0.9 %copy.12 = f32[3,80,8,128]{3,2,1,0:T(8,128)} copy(f32[3,80,8,128]{3,2,1,0:T(8,128)S(1)} %window.1) | data formatting | bytes 1966080

commit v4 on v3

--- a/solution.py
+++ b/solution.py
@@ -23,10 +23,11 @@
 F32 = jnp.float32
 BF16 = jnp.bfloat16
 
-BANDS = (-3, 3, -2, 2, -1, 1, 0)
+BANDS = (-2, 2, -3, 3, -1, 1, 0)
 SECTORS = (-1, 1, 0)
 OFFSETS = [(dl, dn) for dl in BANDS for dn in SECTORS]
-SIDES = [(0, -1), (0, 1), (-1, -1), (-1, 1), (1, -1), (1, 1)]
+SIDES = [(0, -1), (0, 1)]
+CORNERS = [(-1, -1), (-1, 1), (1, -1), (1, 1)]
 
 
 def lanes_of(x, index):
@@ -63,6 +64,8 @@
     ns_recv,
     ew_send,
     ew_recv,
+    corner_send,
+    corner_recv,
     lab_send,
     lab_recv,
     obs_send,
@@ -75,6 +78,8 @@
     ns_rsem,
     ew_ssem,
     ew_rsem,
+    corner_ssem,
+    corner_rsem,
     lab_ssem,
     lab_rsem,
     obs_ssem,
@@ -112,17 +117,17 @@
     ):
         ins.append(pltpu.make_async_copy(src, dst, small_sem.at[i]))
         ins[-1].start()
-    fields_in = []
-    for f in range(3):
-        for r in range(ROWS):
-            copy = pltpu.make_async_copy(
-                state_hbm.at[f, :, r, :], state.at[f, r], state_sem.at[f, r]
-            )
+    rows_in = {}
+    for r in (0, 1, 2, 7, 6, 5, 3, 4):
+        rows_in[r] = [
+            pltpu.make_async_copy(state_hbm.at[f, :, r, :], state.at[f, r], state_sem.at[f, r])
+            for f in range(3)
+        ]
+        for copy in rows_in[r]:
             copy.start()
-            fields_in.append(copy)
 
     barrier = pltpu.get_barrier_semaphore()
-    for dl in BANDS:
+    for dl in (-1, 1, 0):
 
         def greet(dl=dl):
             for dn in SECTORS:
@@ -132,13 +137,9 @@
         if_band(dl, greet)
 
     def met_all():
-        def meet(bands):
-            pl.semaphore_wait(barrier, 2 + 3 * bands)
-
-        for k in range(REACH):
-            pl.when(li == k)(lambda k=k: meet(REACH + k))
-            pl.when(li == n_lat - 1 - k)(lambda k=k: meet(REACH + k))
-        pl.when((li >= REACH) & (li < n_lat - REACH))(lambda: meet(2 * REACH))
+        inner = (li > 0) & (li < n_lat - 1)
+        pl.when(inner)(lambda: pl.semaphore_wait(barrier, 8))
+        pl.when(jnp.logical_not(inner))(lambda: pl.semaphore_wait(barrier, 5))
 
     for g, dl in enumerate(BANDS):
 
@@ -151,7 +152,8 @@
                 for t in range(SUB // 2):
                     ns_recv[t, (1 - dl) // 2] = jnp.zeros(ns_recv.shape[2:], BF16)
                     for dn in (-1, 1):
-                        ew_recv[t, SIDES.index((-dl, dn))] = jnp.zeros(ew_recv.shape[2:], BF16)
+                        i = CORNERS.index((-dl, dn))
+                        corner_recv[t, i] = jnp.zeros((SLOTS, COLS), BF16)
 
         unless_band(dl, clear)
 
@@ -177,6 +179,7 @@
     lon_cols = jnp.where(row_lane < SLOTS, lon_cols, 0)
 
     slot_of = lax.broadcasted_iota(jnp.int32, (SLOTS, COLS), 0)
+    slot_lane = lax.broadcasted_iota(jnp.int32, (SLOTS, COLS), 1)
     picks = []
     for b in range(2):
         live = (batch_row == b).astype(jnp.int32)
@@ -210,8 +213,9 @@
     lab_send[...] = label_tile
     lab_recv[PAIRS - 1] = label_tile
 
-    def send_to_all(src, land, ssem, rsem):
-        for g, dl in enumerate(BANDS):
+    def send_to_all(src, land, ssem, rsem, bands=BANDS):
+        for dl in bands:
+            g = BANDS.index(dl)
 
             def send(g=g, dl=dl):
                 for dn in SECTORS:
@@ -337,13 +341,18 @@
             tile_lane == COLS - 2, second_last, jnp.where(tile_lane == 1, second, ends)
         )
 
+    def labels_to(bands):
+        send_to_all(lab_send, lab_recv, lab_ssem, lab_rsem, bands)
+
     for t in range(SUB // 2):
-        if t == 0:
-            for copy in fields_in:
-                copy.wait()
         packed = jnp.zeros((MEMBERS, COLS), F32)
-
-        def velocities(r, packed):
+        corner_tiles = [jnp.zeros((MEMBERS, COLS), F32) for _ in range(2)]
+
+        def velocities(r):
+            if t == 0:
+                for q in (r - 1, r, r + 1):
+                    for copy in rows_in.pop(q, ()):
+                        copy.wait()
             h, u, v = state[0, r], state[1, r], state[2, r]
             left, right = rolled(h, 1), rolled(h, -1)
             turn = coriolis(r)
@@ -356,7 +365,7 @@
                 new_v = new_v - half * state[0, r + 1]
             state[1, r] = new_u
             state[2, r] = new_v
-            return put(packed, r, middle(new_u, right, left))
+            return middle(new_u, right, left)
 
         def heights(r):
             h = state[0, r]
@@ -366,7 +375,19 @@
             work[r] = h - depth(r) * around
 
         for r in (0, 1, 2, 7, 6, 5):
-            packed = velocities(r, packed)
+            ends = velocities(r)
+            packed = put(packed, r, ends)
+            if r in (0, 1):
+                corner_tiles[0] = put(corner_tiles[0], r, ends)
+            if r in (bottom, bottom - 1):
+                corner_tiles[1] = put(corner_tiles[1], bottom - r, ends)
+        for side, outer in ((0, 0), (1, bottom)):
+            tile = put(put(corner_tiles[side], 2, state[2, outer]), 3, state[0, outer])
+            folded = tile[:SLOTS]
+            for g in range(1, MEMBERS // SLOTS):
+                part = rolled(tile[g * SLOTS : (g + 1) * SLOTS], 16 * g)
+                folded = jnp.where((slot_lane >> 4) == g, part, folded)
+            corner_send[t, side] = folded.astype(BF16)
         for r in (0, 1, 7, 6):
             heights(r)
         for side, outer, inner, sign in ((0, 0, 1, -half), (1, bottom, bottom - 1, half)):
@@ -381,6 +402,17 @@
         if t == 0:
             met_all()
         copies = []
+        for i, (dl, dn) in enumerate(CORNERS):
+            copy = pltpu.make_async_remote_copy(
+                src_ref=corner_send.at[t, (1 + dl) // 2],
+                dst_ref=corner_recv.at[t, i],
+                send_sem=corner_ssem.at[t, i],
+                recv_sem=corner_rsem.at[t, i],
+                device_id=at(dl, dn),
+                device_id_type=MESH,
+            )
+            if_band(dl, copy.start)
+            copies.append((copy, dl, -dl))
         for side, dl in ((0, -1), (1, 1)):
             rows = pl.ds(0, 4 * MEMBERS + (16 if t == 0 else 0))
             copy = pltpu.make_async_remote_copy(
@@ -394,7 +426,7 @@
             if_band(dl, copy.start)
             copies.append((copy, dl, -dl))
         for r in (3, 4):
-            packed = velocities(r, packed)
+            packed = put(packed, r, velocities(r))
         for r in (2, 3, 4, 5):
             heights(r)
         for r in range(ROWS):
@@ -403,8 +435,6 @@
             second = state[1, r] + coriolis(r) * state[2, r]
             second = second + jnp.where(final, half * left, -half * right)
             packed = put(packed, ROWS + r, middle(second, right, left))
-        for i, x in enumerate((state[2, 0], state[2, bottom], state[0, 0], state[0, bottom])):
-            packed = put(packed, 2 * ROWS + i, x)
         ew_send[t, :MEMBERS] = packed.astype(BF16)
         if t == 0:
             rows = jnp.concatenate([half * still[...], zeros8], axis=0)
@@ -422,18 +452,15 @@
             if_band(dl, copy.start)
             copies.append((copy, dl, -dl))
         sent.extend(copies)
-        if t == 0:
-            send_to_all(lab_send, lab_recv, lab_ssem, lab_rsem)
-        if t == 1:
-            all_received(lab_recv, lab_ssem, lab_rsem)
-            make_locality(0)
+        labels_to((-1, 1, 0) if t == 0 else (-2, 2))
         for copy, _, dl in copies:
             if_band(dl, copy.wait_recv)
-
-        def from_ends(dl):
-            west = ew_recv[t, SIDES.index((-dl, 1)), :MEMBERS].astype(F32)
-            east = ew_recv[t, SIDES.index((-dl, -1)), :MEMBERS].astype(F32)
-            return jnp.where((tile_lane & 2) == 0, west, east)
+        if t == SUB // 2 - 1:
+            labels_to((-3, 3))
+
+        def merged(west, east):
+            lane = lax.broadcasted_iota(jnp.int32, west.shape, 1)
+            return jnp.where((lane & 2) == 0, west.astype(F32), east.astype(F32))
 
         def from_rows(side):
             x = [ns_recv[t, side, i * MEMBERS : (i + 1) * MEMBERS].astype(F32) for i in range(4)]
@@ -455,16 +482,20 @@
             for k in (1, 2)
         )
         corners = {}
-        for name, dl, outer, inner, k in (("n", -1, bottom, bottom - 1, 1), ("s", 1, 0, 1, 0)):
-            x = from_ends(dl)
-            v, h = 4 * (2 * ROWS + k), 4 * (2 * ROWS + 2 + k)
+        for name, dl in (("n", -1), ("s", 1)):
+            folded = merged(
+                *(corner_recv[t, CORNERS.index((-dl, dn))] for dn in (1, -1))
+            )
+            x = jnp.concatenate(
+                [folded] + [rolled(folded, -16 * g) for g in range(1, MEMBERS // SLOTS)], axis=0
+            )
             corners[name] = (
-                at_ends(x, 4 * outer, 4 * outer + 3),
-                at_four(x, 4 * outer + 1, 4 * outer, 4 * outer + 3, 4 * outer + 2),
-                at_four(x, 4 * inner + 1, 4 * inner, 4 * inner + 3, 4 * inner + 2),
-                at_ends(x, v + 1, v + 2),
-                at_ends(x, v, v + 3),
-                at_ends(x, h, h + 3),
+                at_ends(x, 0, 3),
+                at_four(x, 1, 0, 3, 2),
+                at_four(x, 5, 4, 7, 6),
+                at_ends(x, 9, 10),
+                at_ends(x, 8, 11),
+                at_ends(x, 12, 15),
             )
         n_h, n_row1, n_row2, n_v, n_v_in, n_h_in = corners["n"]
         s_h, s_row1, s_row2, s_v, s_v_in, s_h_in = corners["s"]
@@ -485,7 +516,7 @@
         south_v2 = south_v2 + half * low * (1.0 - half * south_d2)
         south_v2 = south_v2 - half * south_d2 * corner * s_row2 - coriolis(ROWS) * edge * s_h
 
-        ends = from_ends(0)
+        ends = merged(*(ew_recv[t, SIDES.index((0, dn)), :MEMBERS] for dn in (1, -1)))
         for r in range(ROWS):
             h = state[0, r]
             a, b = 4 * r, 4 * (ROWS + r)
@@ -584,7 +615,8 @@
     send_observations(0)
     for f in range(3):
         make_dev(f)
-    make_locality(1)
+    all_received(lab_recv, lab_ssem, lab_rsem)
+    make_locality(0)
     obs_dev, weights = receive(0)
     update(0, 0, obs_dev, weights, False)
     send_observations(1)
@@ -592,6 +624,7 @@
         update(0, f, obs_dev, weights, False)
     for f in range(3):
         make_dev(f)
+    make_locality(1)
     obs_dev, weights = receive(1)
     for f in range(3):
         update(1, f, obs_dev, weights, True)
@@ -631,6 +664,8 @@
             vmem((SUB // 2, 2, 4 * MEMBERS + 16, COLS), BF16),
             vmem((SUB // 2, MEMBERS + 16, COLS), BF16),
             vmem((SUB // 2, len(SIDES), MEMBERS + 16, COLS), BF16),
+            vmem((SUB // 2, 2, SLOTS, COLS), BF16),
+            vmem((SUB // 2, len(CORNERS), SLOTS, COLS), BF16),
             vmem((SLOTS, COLS), BF16),
             vmem((PAIRS, SLOTS, COLS), BF16),
             vmem((2, SLOTS, COLS), BF16),
@@ -643,6 +678,8 @@
             dma((SUB // 2, 2)),
             dma((SUB // 2, len(SIDES))),
             dma((SUB // 2, len(SIDES))),
+            dma((SUB // 2, len(CORNERS))),
+            dma((SUB // 2, len(CORNERS))),
             dma((len(BANDS),)),
             dma((len(BANDS),)),
             dma((2, len(BANDS))),

time: 40.7 us -> 38 us (0.934)
  Pallas kernels: 39.5 us -> 36.8 us
    pallas_call x1, Pallas kernels: 39.5 us -> 36.8 us  [per_device(): pl.pallas_call(functools.partial(kernel, n_lat, n_lon), out_shape=vmem(ar...]
where the time goes in v4:
time: 38 us; the launch traced here: 37.8 us
  Pallas kernels  36.8 us (97%)
  local copies, waits for them, and re-layouts  0.95 us (2%)
    pallas_call x1, Pallas kernels, per_device(): pl.pallas_call(functools.partial(kernel, n_lat, n_lon), out_shape=vmem(ar...  36.8 us
    unnamed x1, local copies, waits for them, and re-layouts  0.95 us

profile of v4, /device:TPU:384, one launch (start us, length us, event | category | flops | bytes accessed | tf_op | source)
XLA Modules:
  0.0 37.8 jit_solution(2668007880788560854)
XLA Ops:
  0.0 36.8 %window.1 = f32[3,80,8,128]{3,2,1,0:T(8,128)S(1)} custom-call(f32[3,80,8,128]{3,2,1,0:T(8,128)} %state_hbm.1, f32[8,128]{1,0:T(8,128)} %still_hbm.1, f32[32]{0:T(128)} %lat_hbm.1, f32[256]{0:T(256)} %lon_hbm.1, s32[16]{0:T(128)} %cell_hbm.1, s32[16]{0:T(128)} %reach_hbm.1, s32[16]{0:T(128)} %lreach_hbm.1, s32[16]{0:T(128)} %batch_hbm.1, f32[16]{0:T(128)} %value_hbm.1, ...), custom_call_target="tpu_custom_call" | custom-call | tf_op jit(solution)/shard_map/window/pallas_call | solution.py:645
  36.8 0.9 %copy.12 = f32[3,80,8,128]{3,2,1,0:T(8,128)} copy(f32[3,80,8,128]{3,2,1,0:T(8,128)S(1)} %window.1) | data formatting | bytes 1966080

commit v5 on v4

--- a/solution.py
+++ b/solution.py
@@ -101,10 +101,30 @@
         if dl != 0:
             pl.when((li + dl < 0) | (li + dl >= n_lat))(act)
 
+    barrier = pltpu.get_barrier_semaphore()
+    for dl in (-1, 1, 0):
+
+        def greet(dl=dl):
+            for dn in SECTORS:
+                if (dl, dn) != (0, 0):
+                    pl.semaphore_signal(barrier, inc=1, device_id=at(dl, dn), device_id_type=MESH)
+
+        if_band(dl, greet)
+
+    still_in = pltpu.make_async_copy(still_hbm, still, small_sem.at[8])
+    still_in.start()
+    rows_in = {}
+    for r in (0, 7, 1, 6, 2, 5, 3, 4):
+        rows_in[r] = [
+            pltpu.make_async_copy(state_hbm.at[f, :, r, :], state.at[f, r], state_sem.at[f, r])
+            for f in range(3)
+        ]
+        for copy in rows_in[r]:
+            copy.start()
+
     ins = []
     for i, (src, dst) in enumerate(
         (
-            (still_hbm, still),
             (lat_hbm, lat_tab),
             (lon_hbm, lon_tab),
             (cell_hbm, cell),
@@ -117,25 +137,6 @@
     ):
         ins.append(pltpu.make_async_copy(src, dst, small_sem.at[i]))
         ins[-1].start()
-    rows_in = {}
-    for r in (0, 1, 2, 7, 6, 5, 3, 4):
-        rows_in[r] = [
-            pltpu.make_async_copy(state_hbm.at[f, :, r, :], state.at[f, r], state_sem.at[f, r])
-            for f in range(3)
-        ]
-        for copy in rows_in[r]:
-            copy.start()
-
-    barrier = pltpu.get_barrier_semaphore()
-    for dl in (-1, 1, 0):
-
-        def greet(dl=dl):
-            for dn in SECTORS:
-                if (dl, dn) != (0, 0):
-                    pl.semaphore_signal(barrier, inc=1, device_id=at(dl, dn), device_id_type=MESH)
-
-        if_band(dl, greet)
-
     def met_all():
         inner = (li > 0) & (li < n_lat - 1)
         pl.when(inner)(lambda: pl.semaphore_wait(barrier, 8))
@@ -160,58 +161,63 @@
     tile_lane = lax.broadcasted_iota(jnp.int32, (MEMBERS, COLS), 1)
     row_lane = lax.broadcasted_iota(jnp.int32, (1, COLS), 1)
 
-    for copy in ins:
-        copy.wait()
-
     def as_row(ref, fill):
         x = ref[...].reshape(1, SLOTS)
         return jnp.concatenate([x, jnp.full((1, COLS - SLOTS), fill, x.dtype)], axis=1)
 
-    cell_row = as_row(cell, 0)
-    reach_row = as_row(reach, 0).astype(F32)
-    lreach_row = as_row(lreach, 0).astype(F32)
-    batch_row = as_row(batch, -1)
-    value_row = as_row(value, 0.0)
-    var_row = as_row(var, 1.0)
-    lat_rows = cell_row // (COLS * n_lon) - li * ROWS
-    lon_cols = lax.rem(cell_row, COLS * n_lon) - lo * COLS
-    lat_rows = jnp.where(row_lane < SLOTS, lat_rows, 0)
-    lon_cols = jnp.where(row_lane < SLOTS, lon_cols, 0)
-
-    slot_of = lax.broadcasted_iota(jnp.int32, (SLOTS, COLS), 0)
-    slot_lane = lax.broadcasted_iota(jnp.int32, (SLOTS, COLS), 1)
-    picks = []
-    for b in range(2):
-        live = (batch_row == b).astype(jnp.int32)
-        upto = live
-        for s in (1, 2, 4, 8):
-            upto = upto + jnp.where(row_lane >= s, pltpu.roll(upto, s, 1), 0)
-        rank = jnp.where(live == 1, upto - 1, -1)
-        picks.append((slot_of == rank).astype(F32).astype(BF16))
-
     sub8 = lax.broadcasted_iota(jnp.int32, (8, COLS), 0)
-    labels = jnp.where(
-        sub8 == 0,
-        lat_rows.astype(F32),
-        jnp.where(
-            sub8 == 1,
-            lon_cols.astype(F32),
-            jnp.where(sub8 == 2, reach_row, jnp.where(sub8 == 3, lreach_row, 0.0)),
-        ),
-    )
     zeros8 = jnp.zeros((8, COLS), F32)
     zeros_rest = jnp.zeros((COLS - 16, COLS), F32)
     rows_to_lanes = (((1,), (1,)), ((), ()))
-    label_tile = 0.0
-    for b in range(2):
-        spread = jnp.concatenate([labels, zeros8] if b == 0 else [zeros8, labels], axis=0)
-        spread = jnp.concatenate([spread, zeros_rest], axis=0).astype(BF16)
-        label_tile = label_tile + lax.dot_general(
-            picks[b], spread, rows_to_lanes, preferred_element_type=F32
+    slot_lane = lax.broadcasted_iota(jnp.int32, (SLOTS, COLS), 1)
+
+    def observed():
+        for copy in ins:
+            copy.wait()
+
+        cell_row = as_row(cell, 0)
+        reach_row = as_row(reach, 0).astype(F32)
+        lreach_row = as_row(lreach, 0).astype(F32)
+        batch_row = as_row(batch, -1)
+        value_row = as_row(value, 0.0)
+        var_row = as_row(var, 1.0)
+        lat_rows = cell_row // (COLS * n_lon) - li * ROWS
+        lon_cols = lax.rem(cell_row, COLS * n_lon) - lo * COLS
+        lat_rows = jnp.where(row_lane < SLOTS, lat_rows, 0)
+        lon_cols = jnp.where(row_lane < SLOTS, lon_cols, 0)
+        return lat_rows, lon_cols, reach_row, lreach_row, batch_row, value_row, var_row
+
+    def make_labels():
+        slot_of = lax.broadcasted_iota(jnp.int32, (SLOTS, COLS), 0)
+        picks = []
+        for b in range(2):
+            live = (batch_row == b).astype(jnp.int32)
+            upto = live
+            for s in (1, 2, 4, 8):
+                upto = upto + jnp.where(row_lane >= s, pltpu.roll(upto, s, 1), 0)
+            rank = jnp.where(live == 1, upto - 1, -1)
+            picks.append((slot_of == rank).astype(F32).astype(BF16))
+
+        labels = jnp.where(
+            sub8 == 0,
+            lat_rows.astype(F32),
+            jnp.where(
+                sub8 == 1,
+                lon_cols.astype(F32),
+                jnp.where(sub8 == 2, reach_row, jnp.where(sub8 == 3, lreach_row, 0.0)),
+            ),
         )
-    label_tile = label_tile.astype(BF16)
-    lab_send[...] = label_tile
-    lab_recv[PAIRS - 1] = label_tile
+        label_tile = 0.0
+        for b in range(2):
+            spread = jnp.concatenate([labels, zeros8] if b == 0 else [zeros8, labels], axis=0)
+            spread = jnp.concatenate([spread, zeros_rest], axis=0).astype(BF16)
+            label_tile = label_tile + lax.dot_general(
+                picks[b], spread, rows_to_lanes, preferred_element_type=F32
+            )
+        label_tile = label_tile.astype(BF16)
+        lab_send[...] = label_tile
+        lab_recv[PAIRS - 1] = label_tile
+        return picks
 
     def send_to_all(src, land, ssem, rsem, bands=BANDS):
         for dl in bands:
@@ -344,9 +350,31 @@
     def labels_to(bands):
         send_to_all(lab_send, lab_recv, lab_ssem, lab_rsem, bands)
 
+    pending = {}
+
+    def finish(*which):
+        for r in which:
+            if r in pending:
+                pending.pop(r)()
+
     for t in range(SUB // 2):
         packed = jnp.zeros((MEMBERS, COLS), F32)
         corner_tiles = [jnp.zeros((MEMBERS, COLS), F32) for _ in range(2)]
+        copies = []
+        rows_copies = []
+        corner_copies = []
+
+        def send(group, src, dst, ssem, rsem, dl, dn):
+            copy = pltpu.make_async_remote_copy(
+                src_ref=src,
+                dst_ref=dst,
+                send_sem=ssem,
+                recv_sem=rsem,
+                device_id=at(dl, dn),
+                device_id_type=MESH,
+            )
+            if_band(dl, copy.start)
+            group.append((copy, dl, -dl))
 
         def velocities(r):
             if t == 0:
@@ -374,57 +402,67 @@
             around = apart(state[1, r], -edge * h) + (below - above)
             work[r] = h - depth(r) * around
 
-        for r in (0, 1, 2, 7, 6, 5):
-            ends = velocities(r)
-            packed = put(packed, r, ends)
-            if r in (0, 1):
-                corner_tiles[0] = put(corner_tiles[0], r, ends)
-            if r in (bottom, bottom - 1):
-                corner_tiles[1] = put(corner_tiles[1], bottom - r, ends)
+        def send_rows(part, rows):
+            for side, dl in ((0, -1), (1, 1)):
+                send(
+                    rows_copies if part else copies,
+                    ns_send.at[t, side, rows],
+                    ns_recv.at[t, side, rows],
+                    ns_ssem.at[t, side, part],
+                    ns_rsem.at[t, side, part],
+                    dl,
+                    0,
+                )
+
+        finish(0, 1, 7, 6)
         for side, outer in ((0, 0), (1, bottom)):
-            tile = put(put(corner_tiles[side], 2, state[2, outer]), 3, state[0, outer])
+            ends = velocities(outer)
+            packed = put(packed, outer, ends)
+            tile = put(corner_tiles[side], 0, ends)
+            tile = put(tile, 2, state[2, outer])
+            corner_tiles[side] = put(tile, 3, state[0, outer])
+            ns_send[t, side, :MEMBERS] = state[0, outer].astype(BF16)
+            ns_send[t, side, MEMBERS : 2 * MEMBERS] = state[2, outer].astype(BF16)
+        if t == 0:
+            met_all()
+        send_rows(0, pl.ds(0, 2 * MEMBERS))
+        finish(2, 5)
+        for side, inner in ((0, 1), (1, bottom - 1)):
+            ends = velocities(inner)
+            packed = put(packed, inner, ends)
+            tile = put(corner_tiles[side], 1, ends)
             folded = tile[:SLOTS]
             for g in range(1, MEMBERS // SLOTS):
                 part = rolled(tile[g * SLOTS : (g + 1) * SLOTS], 16 * g)
                 folded = jnp.where((slot_lane >> 4) == g, part, folded)
             corner_send[t, side] = folded.astype(BF16)
+        for i, (dl, dn) in enumerate(CORNERS):
+            send(
+                corner_copies,
+                corner_send.at[t, (1 + dl) // 2],
+                corner_recv.at[t, i],
+                corner_ssem.at[t, i],
+                corner_rsem.at[t, i],
+                dl,
+                dn,
+            )
+        finish(3, 4)
+        for r in (2, 5):
+            packed = put(packed, r, velocities(r))
+        if t == 0:
+            still_in.wait()
         for r in (0, 1, 7, 6):
             heights(r)
         for side, outer, inner, sign in ((0, 0, 1, -half), (1, bottom, bottom - 1, half)):
             second = state[2, outer] - coriolis(outer) * state[1, outer] + sign * work[inner]
-            for i, x in enumerate((state[0, outer], state[2, outer], work[outer], second)):
-                ns_send[t, side, i * MEMBERS : (i + 1) * MEMBERS] = x.astype(BF16)
+            ns_send[t, side, 2 * MEMBERS : 3 * MEMBERS] = work[outer].astype(BF16)
+            ns_send[t, side, 3 * MEMBERS : 4 * MEMBERS] = second.astype(BF16)
             if t == 0:
                 rows = jnp.concatenate(
                     [depth(outer), depth(inner), jnp.zeros((14, COLS), F32)], axis=0
                 )
                 ns_send[t, side, 4 * MEMBERS :] = rows.astype(BF16)
-        if t == 0:
-            met_all()
-        copies = []
-        for i, (dl, dn) in enumerate(CORNERS):
-            copy = pltpu.make_async_remote_copy(
-                src_ref=corner_send.at[t, (1 + dl) // 2],
-                dst_ref=corner_recv.at[t, i],
-                send_sem=corner_ssem.at[t, i],
-                recv_sem=corner_rsem.at[t, i],
-                device_id=at(dl, dn),
-                device_id_type=MESH,
-            )
-            if_band(dl, copy.start)
-            copies.append((copy, dl, -dl))
-        for side, dl in ((0, -1), (1, 1)):
-            rows = pl.ds(0, 4 * MEMBERS + (16 if t == 0 else 0))
-            copy = pltpu.make_async_remote_copy(
-                src_ref=ns_send.at[t, side, rows],
-                dst_ref=ns_recv.at[t, side, rows],
-                send_sem=ns_ssem.at[t, side],
-                recv_sem=ns_rsem.at[t, side],
-                device_id=at(dl, 0),
-                device_id_type=MESH,
-            )
-            if_band(dl, copy.start)
-            copies.append((copy, dl, -dl))
+        send_rows(1, pl.ds(2 * MEMBERS, 2 * MEMBERS + (16 if t == 0 else 0)))
         for r in (3, 4):
             packed = put(packed, r, velocities(r))
         for r in (2, 3, 4, 5):
@@ -441,34 +479,36 @@
             ew_send[t, MEMBERS:] = rows.astype(BF16)
         for i, (dl, dn) in enumerate(SIDES):
             rows = pl.ds(0, MEMBERS + (16 if t == 0 else 0))
-            copy = pltpu.make_async_remote_copy(
-                src_ref=ew_send.at[t, rows],
-                dst_ref=ew_recv.at[t, i, rows],
-                send_sem=ew_ssem.at[t, i],
-                recv_sem=ew_rsem.at[t, i],
-                device_id=at(dl, dn),
-                device_id_type=MESH,
+            send(
+                copies,
+                ew_send.at[t, rows],
+                ew_recv.at[t, i, rows],
+                ew_ssem.at[t, i],
+                ew_rsem.at[t, i],
+                dl,
+                dn,
             )
-            if_band(dl, copy.start)
-            copies.append((copy, dl, -dl))
-        sent.extend(copies)
+        sent.extend(copies + rows_copies + corner_copies)
+        if t == 0:
+            (lat_rows, lon_cols, reach_row, lreach_row, batch_row, value_row, var_row) = observed()
+            picks = make_labels()
         labels_to((-1, 1, 0) if t == 0 else (-2, 2))
         for copy, _, dl in copies:
             if_band(dl, copy.wait_recv)
-        if t == SUB // 2 - 1:
-            labels_to((-3, 3))
 
         def merged(west, east):
             lane = lax.broadcasted_iota(jnp.int32, west.shape, 1)
             return jnp.where((lane & 2) == 0, west.astype(F32), east.astype(F32))
 
-        def from_rows(side):
-            x = [ns_recv[t, side, i * MEMBERS : (i + 1) * MEMBERS].astype(F32) for i in range(4)]
+        def from_rows(side, i):
+            return ns_recv[t, side, i * MEMBERS : (i + 1) * MEMBERS].astype(F32)
+
+        def edge_depths(side):
             rows = ns_recv[0, side, 4 * MEMBERS :].astype(F32)
-            return x + [rows[0:1], rows[1:2]]
-
-        south_h, south_v, south_h1, south_v2, south_d1, south_d2 = from_rows(0)
-        north_h, north_v, north_h1, north_v2, north_d1, north_d2 = from_rows(1)
+            return rows[0:1], rows[1:2]
+
+        south_h, south_v = from_rows(0, 0), from_rows(0, 1)
+        north_h, north_v = from_rows(1, 0), from_rows(1, 1)
         ends_d = [
             ew_recv[0, SIDES.index((0, dn)), MEMBERS:].astype(F32)[:ROWS] for dn in (1, -1)
         ]
@@ -481,6 +521,34 @@
             )
             for k in (1, 2)
         )
+        top, low = state[0, 0], state[0, bottom]
+        top_v = state[2, 0] + half * north_h
+        low_v = state[2, bottom] - half * south_h
+        state[2, 0] = top_v
+        state[2, bottom] = low_v
+        north_v = (north_v - half * top) * north_live
+        south_v = (south_v + half * low) * south_live
+        ends = merged(*(ew_recv[t, SIDES.index((0, dn)), :MEMBERS] for dn in (1, -1)))
+        for r in range(ROWS):
+            h = state[0, r]
+            a, b = 4 * r, 4 * (ROWS + r)
+            far_h = at_ends(ends, a, a + 3)
+            far_u = at_ends(ends, a + 1, a + 2)
+            far_h1 = at_ends(ends, b, b + 3)
+            far_u2 = at_ends(ends, b + 1, b + 2)
+            u = state[1, r] + edge * far_h
+            state[1, r] = u
+            above = state[2, r - 1] if r > 0 else north_v
+            below = state[2, r + 1] if r < bottom else south_v
+            work[r] = h - depth(r) * (apart(u, far_u - edge * h) + (below - above))
+            end_d1, end_d2 = d1[r : r + 1], d2[r : r + 1]
+            outside[0, r] = far_h1 - end_d1 * (edge * (1.0 / half) * u - half * far_h)
+            outside[1, r] = far_u2 - edge * h * (1.0 - half * end_d2)
+
+        for copy, _, dl in corner_copies + rows_copies:
+            if_band(dl, copy.wait_recv)
+        if t == SUB // 2 - 1:
+            labels_to((-3, 3))
         corners = {}
         for name, dl in (("n", -1), ("s", 1)):
             folded = merged(
@@ -499,14 +567,10 @@
             )
         n_h, n_row1, n_row2, n_v, n_v_in, n_h_in = corners["n"]
         s_h, s_row1, s_row2, s_v, s_v_in, s_h_in = corners["s"]
-
-        top, low = state[0, 0], state[0, bottom]
-        top_v = state[2, 0] + half * north_h
-        low_v = state[2, bottom] - half * south_h
-        state[2, 0] = top_v
-        state[2, bottom] = low_v
-        north_v = (north_v - half * top) * north_live
-        south_v = (south_v + half * low) * south_live
+        south_h1, south_v2 = from_rows(0, 2), from_rows(0, 3)
+        north_h1, north_v2 = from_rows(1, 2), from_rows(1, 3)
+        south_d1, south_d2 = edge_depths(0)
+        north_d1, north_d2 = edge_depths(1)
         north_h1 = north_h1 - north_d1 * (top_v - half * north_h) + north_d1 * corner * n_row1
         south_h1 = south_h1 + south_d1 * (low_v + half * south_h) + south_d1 * corner * s_row1
         north_h1 = north_h1 * north_live
@@ -515,38 +579,15 @@
         north_v2 = north_v2 + half * north_d2 * corner * n_row2 - coriolis(-1) * edge * n_h
         south_v2 = south_v2 + half * low * (1.0 - half * south_d2)
         south_v2 = south_v2 - half * south_d2 * corner * s_row2 - coriolis(ROWS) * edge * s_h
-
-        ends = merged(*(ew_recv[t, SIDES.index((0, dn)), :MEMBERS] for dn in (1, -1)))
-        for r in range(ROWS):
-            h = state[0, r]
-            a, b = 4 * r, 4 * (ROWS + r)
-            far_h = at_ends(ends, a, a + 3)
-            far_u = at_ends(ends, a + 1, a + 2)
-            far_h1 = at_ends(ends, b, b + 3)
-            far_u2 = at_ends(ends, b + 1, b + 2)
-            u = state[1, r] + edge * far_h
-            state[1, r] = u
-            above = state[2, r - 1] if r > 0 else north_v
-            below = state[2, r + 1] if r < bottom else south_v
-            work[r] = h - depth(r) * (apart(u, far_u - edge * h) + (below - above))
-            end_d1, end_d2 = d1[r : r + 1], d2[r : r + 1]
-            far_h1 = far_h1 - end_d1 * (edge * (1.0 / half) * u - half * far_h)
-            far_u2 = far_u2 - edge * h * (1.0 - half * end_d2)
-            if r == 0:
-                far_h1 = far_h1 + end_d1 * n_v
-                far_u2 = far_u2 + coriolis(r) * half * n_h + edge * end_d2 * n_v_in
-            if r == 1:
-                far_h1 = far_h1 + half * end_d1 * n_h
-                far_u2 = far_u2 + half * edge * end_d2 * n_h_in
-            if r == bottom - 1:
-                far_h1 = far_h1 + half * end_d1 * s_h
-                far_u2 = far_u2 + half * edge * end_d2 * s_h_in
-            if r == bottom:
-                far_h1 = far_h1 - end_d1 * s_v
-                far_u2 = far_u2 - coriolis(r) * half * s_h - edge * end_d2 * s_v_in
-            outside[0, r] = far_h1
-            outside[1, r] = far_u2
-        for r in range(ROWS):
+        for r, far_h1, far_u2 in (
+            (0, n_v, coriolis(0) * half * n_h + edge * d2[0:1] * n_v_in),
+            (1, half * n_h, half * edge * d2[1:2] * n_h_in),
+            (6, half * s_h, half * edge * d2[6:7] * s_h_in),
+            (7, -s_v, -coriolis(7) * half * s_h - edge * d2[7:8] * s_v_in),
+        ):
+            outside[0, r] = outside[0, r] + d1[r : r + 1] * far_h1
+            outside[1, r] = outside[1, r] + far_u2
+        for r in (0, 1, 7, 6, 2, 5, 3, 4):
             h, u, v = work[r], state[1, r], state[2, r]
             above = work[r - 1] if r > 0 else north_h1
             below = work[r + 1] if r < bottom else south_h1
@@ -554,12 +595,18 @@
             state[2, r] = v - coriolis(r) * u - half * (below - above)
         north_v2 = (north_v2 - half * work[0]) * north_live
         south_v2 = (south_v2 + half * work[bottom]) * south_live
-        for r in range(ROWS):
+
+        def last_height(r, north_v2, south_v2):
             h = work[r]
             above = state[2, r - 1] if r > 0 else north_v2
             below = state[2, r + 1] if r < bottom else south_v2
             around = apart(state[1, r], outside[1, r] - edge * h) + (below - above)
             state[0, r] = h - depth(r) * around
+
+        for r in range(ROWS):
+            pending[r] = functools.partial(last_height, r, north_v2, south_v2)
+
+    finish(*range(ROWS))
 
     pick_lane = jnp.broadcast_to(lon_cols, (MEMBERS, COLS))
 
@@ -674,8 +721,8 @@
             vmem((3, MEMBERS, ROWS * COLS), BF16),
             dma((9,)),
             dma((3, ROWS)),
-            dma((SUB // 2, 2)),
-            dma((SUB // 2, 2)),
+            dma((SUB // 2, 2, 2)),
+            dma((SUB // 2, 2, 2)),
             dma((SUB // 2, len(SIDES))),
             dma((SUB // 2, len(SIDES))),
             dma((SUB // 2, len(CORNERS))),

time: 38 us -> 36.7 us (0.966)
  Pallas kernels: 36.8 us -> 35.5 us
    pallas_call x1, Pallas kernels: 36.8 us -> 35.5 us  [per_device(): pl.pallas_call(functools.partial(kernel, n_lat, n_lon), out_shape=vmem(ar...]
where the time goes in v5:
time: 36.7 us; the launch traced here: 36.5 us
  Pallas kernels  35.5 us (97%)
  local copies, waits for them, and re-layouts  0.95 us (3%)
    pallas_call x1, Pallas kernels, per_device(): pl.pallas_call(functools.partial(kernel, n_lat, n_lon), out_shape=vmem(ar...  35.5 us
    unnamed x1, local copies, waits for them, and re-layouts  0.95 us

profile of v5, /device:TPU:384, one launch (start us, length us, event | category | flops | bytes accessed | tf_op | source)
XLA Modules:
  0.0 36.5 jit_solution(12225464018546712756)
XLA Ops:
  0.0 35.5 %window.1 = f32[3,80,8,128]{3,2,1,0:T(8,128)S(1)} custom-call(f32[3,80,8,128]{3,2,1,0:T(8,128)} %state_hbm.1, f32[8,128]{1,0:T(8,128)} %still_hbm.1, f32[32]{0:T(128)} %lat_hbm.1, f32[256]{0:T(256)} %lon_hbm.1, s32[16]{0:T(128)} %cell_hbm.1, s32[16]{0:T(128)} %reach_hbm.1, s32[16]{0:T(128)} %lreach_hbm.1, s32[16]{0:T(128)} %batch_hbm.1, f32[16]{0:T(128)} %value_hbm.1, ...), custom_call_target="tpu_custom_call" | custom-call | tf_op jit(solution)/shard_map/window/pallas_call | solution.py:692
  35.5 0.9 %copy.12 = f32[3,80,8,128]{3,2,1,0:T(8,128)} copy(f32[3,80,8,128]{3,2,1,0:T(8,128)S(1)} %window.1) | data formatting | bytes 1966080

commit v6 on v5

--- a/solution.py
+++ b/solution.py
@@ -645,11 +645,13 @@
         return obs_dev, weights
 
     def update(b, f, obs_dev, weights, last):
+        gains = []
+        for r in range(ROWS):
+            lanes = slice(r * COLS, (r + 1) * COLS)
+            cov = jnp.dot(obs_dev, dev[f, :, lanes], preferred_element_type=F32)
+            gains.append((cov * loc[b, r]).astype(BF16))
         for pair in range(ROWS // 2):
-            lanes = slice(2 * pair * COLS, 2 * (pair + 1) * COLS)
-            cov = jnp.dot(obs_dev, dev[f, :, lanes], preferred_element_type=F32)
-            taper = jnp.concatenate([loc[b, 2 * pair], loc[b, 2 * pair + 1]], axis=1)
-            gain = (cov * taper).astype(BF16)
+            gain = jnp.concatenate(gains[2 * pair : 2 * pair + 2], axis=1)
             step = jnp.dot(weights, gain, preferred_element_type=F32)
             for i in range(2):
                 r = 2 * pair + i

time: 36.7 us -> 34.8 us (0.948)
  Pallas kernels: 35.5 us -> 33.7 us
    pallas_call x1, Pallas kernels: 35.5 us -> 33.7 us  [per_device(): pl.pallas_call(functools.partial(kernel, n_lat, n_lon), out_shape=vmem(ar...]
where the time goes in v6:
time: 34.8 us; the launch traced here: 34.6 us
  Pallas kernels  33.7 us (97%)
  local copies, waits for them, and re-layouts  0.95 us (3%)
    pallas_call x1, Pallas kernels, per_device(): pl.pallas_call(functools.partial(kernel, n_lat, n_lon), out_shape=vmem(ar...  33.7 us
    unnamed x1, local copies, waits for them, and re-layouts  0.95 us

profile of v6, /device:TPU:384, one launch (start us, length us, event | category | flops | bytes accessed | tf_op | source)
XLA Modules:
  0.0 34.6 jit_solution(6619200029138586003)
XLA Ops:
  0.0 33.7 %window.1 = f32[3,80,8,128]{3,2,1,0:T(8,128)S(1)} custom-call(f32[3,80,8,128]{3,2,1,0:T(8,128)} %state_hbm.1, f32[8,128]{1,0:T(8,128)} %still_hbm.1, f32[32]{0:T(128)} %lat_hbm.1, f32[256]{0:T(256)} %lon_hbm.1, s32[16]{0:T(128)} %cell_hbm.1, s32[16]{0:T(128)} %reach_hbm.1, s32[16]{0:T(128)} %lreach_hbm.1, s32[16]{0:T(128)} %batch_hbm.1, f32[16]{0:T(128)} %value_hbm.1, ...), custom_call_target="tpu_custom_call" | custom-call | tf_op jit(solution)/shard_map/window/pallas_call | solution.py:694
  33.7 0.9 %copy.12 = f32[3,80,8,128]{3,2,1,0:T(8,128)} copy(f32[3,80,8,128]{3,2,1,0:T(8,128)S(1)} %window.1) | data formatting | bytes 1966080

commit v7 on v6

--- a/solution.py
+++ b/solution.py
@@ -113,14 +113,13 @@
 
     still_in = pltpu.make_async_copy(still_hbm, still, small_sem.at[8])
     still_in.start()
+    order = [(f, r) for r, q in ((0, 1), (7, 6)) for f, r in ((0, r), (1, r), (2, r), (0, q))]
+    order += [(f, r) for r in (1, 6, 2, 5, 3, 4) for f in range(3) if (f, r) not in order]
     rows_in = {}
-    for r in (0, 7, 1, 6, 2, 5, 3, 4):
-        rows_in[r] = [
-            pltpu.make_async_copy(state_hbm.at[f, :, r, :], state.at[f, r], state_sem.at[f, r])
-            for f in range(3)
-        ]
-        for copy in rows_in[r]:
-            copy.start()
+    for f, r in order:
+        copy = pltpu.make_async_copy(state_hbm.at[f, :, r, :], state.at[f, r], state_sem.at[f, r])
+        copy.start()
+        rows_in[f, r] = copy
 
     ins = []
     for i, (src, dst) in enumerate(
@@ -378,9 +377,9 @@
 
         def velocities(r):
             if t == 0:
-                for q in (r - 1, r, r + 1):
-                    for copy in rows_in.pop(q, ()):
-                        copy.wait()
+                for key in ((0, r - 1), (0, r), (0, r + 1), (1, r), (2, r)):
+                    if key in rows_in:
+                        rows_in.pop(key).wait()
             h, u, v = state[0, r], state[1, r], state[2, r]
             left, right = rolled(h, 1), rolled(h, -1)
             turn = coriolis(r)
@@ -495,6 +494,8 @@
         labels_to((-1, 1, 0) if t == 0 else (-2, 2))
         for copy, _, dl in copies:
             if_band(dl, copy.wait_recv)
+        if t == SUB // 2 - 1:
+            labels_to((-3, 3))
 
         def merged(west, east):
             lane = lax.broadcasted_iota(jnp.int32, west.shape, 1)
@@ -547,8 +548,6 @@
 
         for copy, _, dl in corner_copies + rows_copies:
             if_band(dl, copy.wait_recv)
-        if t == SUB // 2 - 1:
-            labels_to((-3, 3))
         corners = {}
         for name, dl in (("n", -1), ("s", 1)):
             folded = merged(
@@ -610,10 +609,13 @@
 
     pick_lane = jnp.broadcast_to(lon_cols, (MEMBERS, COLS))
 
-    def send_observations(b):
-        prior = jnp.zeros((MEMBERS, COLS), F32)
+    def at_observed(tile_of_row, lane):
+        found = jnp.zeros(lane.shape, F32)
         for r in range(ROWS):
-            prior = jnp.where(lat_rows == r, lanes_of(state[0, r], pick_lane), prior)
+            found = jnp.where(lat_rows == r, lanes_of(tile_of_row(r), lane), found)
+        return found
+
+    def send_observations(b, prior):
         mean = jnp.sum(prior, axis=0, keepdims=True) / MEMBERS
         away = prior - mean
         total = jnp.sum(away * away, axis=0, keepdims=True) / (MEMBERS - 1) + var_row
@@ -628,6 +630,7 @@
         obs_send[b] = tile
         obs_recv[b, PAIRS - 1] = tile
         send_to_all(obs_send.at[b], obs_recv.at[b], obs_ssem.at[b], obs_rsem.at[b])
+        return away.astype(BF16)
 
     def make_dev(f):
         for r in range(ROWS):
@@ -661,28 +664,30 @@
                 else:
                     state[f, r] = new
 
-    send_observations(0)
+    prior = at_observed(lambda r: state[0, r], pick_lane)
+    prior_dev = send_observations(0, prior)
     for f in range(3):
         make_dev(f)
     all_received(lab_recv, lab_ssem, lab_rsem)
     make_locality(0)
+    prior_loc = at_observed(lambda r: loc[0, r], jnp.broadcast_to(lon_cols, (OBS, COLS)))
     obs_dev, weights = receive(0)
-    update(0, 0, obs_dev, weights, False)
-    send_observations(1)
-    for f in (1, 2):
+    cov = jnp.dot(obs_dev, prior_dev, preferred_element_type=F32)
+    gain = (cov * prior_loc).astype(BF16)
+    send_observations(1, prior + jnp.dot(weights, gain, preferred_element_type=F32))
+    for f in range(3):
         update(0, f, obs_dev, weights, False)
     for f in range(3):
         make_dev(f)
     make_locality(1)
-    obs_dev, weights = receive(1)
-    for f in range(3):
-        update(1, f, obs_dev, weights, True)
-
     for copy, dl, _ in sent:
         if_band(dl, copy.wait_send)
     all_sent(lab_recv, lab_ssem, lab_rsem)
     for b in range(2):
         all_sent(obs_recv.at[b], obs_ssem.at[b], obs_rsem.at[b])
+    obs_dev, weights = receive(1)
+    for f in range(3):
+        update(1, f, obs_dev, weights, True)
 
 
 def per_device(n_lat, n_lon, *args):

time: 34.8 us -> 34.6 us (level)
  no operation moved by 1% of the time
where the time goes in v7:
time: 34.6 us; the launch traced here: 34.4 us
  Pallas kernels  33.5 us (97%)
  local copies, waits for them, and re-layouts  0.95 us (3%)
    pallas_call x1, Pallas kernels, per_device(): pl.pallas_call(functools.partial(kernel, n_lat, n_lon), out_shape=vmem(ar...  33.5 us
    unnamed x1, local copies, waits for them, and re-layouts  0.95 us

profile of v7, /device:TPU:384, one launch (start us, length us, event | category | flops | bytes accessed | tf_op | source)
XLA Modules:
  0.0 34.4 jit_solution(15246987695001109119)
XLA Ops:
  0.0 33.5 %window.1 = f32[3,80,8,128]{3,2,1,0:T(8,128)S(1)} custom-call(f32[3,80,8,128]{3,2,1,0:T(8,128)} %state_hbm.1, f32[8,128]{1,0:T(8,128)} %still_hbm.1, f32[32]{0:T(128)} %lat_hbm.1, f32[256]{0:T(256)} %lon_hbm.1, s32[16]{0:T(128)} %cell_hbm.1, s32[16]{0:T(128)} %reach_hbm.1, s32[16]{0:T(128)} %lreach_hbm.1, s32[16]{0:T(128)} %batch_hbm.1, f32[16]{0:T(128)} %value_hbm.1, ...), custom_call_target="tpu_custom_call" | custom-call | tf_op jit(solution)/shard_map/window/pallas_call | solution.py:699
  33.5 0.9 %copy.12 = f32[3,80,8,128]{3,2,1,0:T(8,128)} copy(f32[3,80,8,128]{3,2,1,0:T(8,128)S(1)} %window.1) | data formatting | bytes 1966080

commit v8 on v7

--- a/solution.py
+++ b/solution.py
@@ -647,12 +647,15 @@
         weights = jnp.transpose(weights).astype(BF16)[:MEMBERS]
         return obs_dev, weights
 
-    def update(b, f, obs_dev, weights, last):
+    def make_gains(b, f, obs_dev):
         gains = []
         for r in range(ROWS):
             lanes = slice(r * COLS, (r + 1) * COLS)
             cov = jnp.dot(obs_dev, dev[f, :, lanes], preferred_element_type=F32)
             gains.append((cov * loc[b, r]).astype(BF16))
+        return gains
+
+    def update(f, gains, weights, last):
         for pair in range(ROWS // 2):
             gain = jnp.concatenate(gains[2 * pair : 2 * pair + 2], axis=1)
             step = jnp.dot(weights, gain, preferred_element_type=F32)
@@ -676,7 +679,7 @@
     gain = (cov * prior_loc).astype(BF16)
     send_observations(1, prior + jnp.dot(weights, gain, preferred_element_type=F32))
     for f in range(3):
-        update(0, f, obs_dev, weights, False)
+        update(f, make_gains(0, f, obs_dev), weights, False)
     for f in range(3):
         make_dev(f)
     make_locality(1)
@@ -686,8 +689,11 @@
     for b in range(2):
         all_sent(obs_recv.at[b], obs_ssem.at[b], obs_rsem.at[b])
     obs_dev, weights = receive(1)
+    gains = make_gains(1, 0, obs_dev)
     for f in range(3):
-        update(1, f, obs_dev, weights, True)
+        ahead = make_gains(1, f + 1, obs_dev) if f < 2 else None
+        update(f, gains, weights, True)
+        gains = ahead
 
 
 def per_device(n_lat, n_lon, *args):

time: 34.6 us -> 34.5 us (level)
  no operation moved by 1% of the time
where the time goes in v8:
time: 34.5 us; the launch traced here: 34.3 us
  Pallas kernels  33.4 us (97%)
  local copies, waits for them, and re-layouts  0.95 us (3%)
    pallas_call x1, Pallas kernels, per_device(): pl.pallas_call(functools.partial(kernel, n_lat, n_lon), out_shape=vmem(ar...  33.4 us
    unnamed x1, local copies, waits for them, and re-layouts  0.95 us

profile of v8, /device:TPU:384, one launch (start us, length us, event | category | flops | bytes accessed | tf_op | source)
XLA Modules:
  0.0 34.3 jit_solution(2727614434831536822)
XLA Ops:
  0.0 33.4 %window.1 = f32[3,80,8,128]{3,2,1,0:T(8,128)S(1)} custom-call(f32[3,80,8,128]{3,2,1,0:T(8,128)} %state_hbm.1, f32[8,128]{1,0:T(8,128)} %still_hbm.1, f32[32]{0:T(128)} %lat_hbm.1, f32[256]{0:T(256)} %lon_hbm.1, s32[16]{0:T(128)} %cell_hbm.1, s32[16]{0:T(128)} %reach_hbm.1, s32[16]{0:T(128)} %lreach_hbm.1, s32[16]{0:T(128)} %batch_hbm.1, f32[16]{0:T(128)} %value_hbm.1, ...), custom_call_target="tpu_custom_call" | custom-call | tf_op jit(solution)/shard_map/window/pallas_call | solution.py:705
  33.4 0.9 %copy.12 = f32[3,80,8,128]{3,2,1,0:T(8,128)} copy(f32[3,80,8,128]{3,2,1,0:T(8,128)S(1)} %window.1) | data formatting | bytes 1966080
